TPU v7x, 32 devices: a whole 2x2x4 slice. The times are simulated.
32 devices in a mesh: rep: 2 (over y), sec: 4 (over x, core), tp: 4 (over z).
Axes of the slice: x: 2, y: 2, z: 4, core: 2. Of those that a mesh axis runs over, the one named last changes fastest.
Arguments:
- resid: bfloat16 [96, 5120], P(('rep', 'tp'), 'sec'), parts along dimension 0, may hold values from -6 to 6
- query: bfloat16 [96, 5120], P(('rep', 'tp'), 'sec'), parts along dimension 0, may hold values from -120 to 120
- new_kv: bfloat16 [96, 2048], P(('rep', 'tp'), 'sec'), parts along dimension 0, may hold values from -4 to 4
- key_cache: bfloat16 [96, 224, 1024], P(('rep', 'sec', 'tp')), parts along dimension 0, may hold values from -4 to 4
- cached_value_rows: bfloat16 [96, 224, 1024], P(('rep', 'sec', 'tp')), parts along dimension 0, may hold values from -6 to 6
- cache_len: int32 [96], P(('rep', 'sec', 'tp')), parts along dimension 0, may hold values from 1 to 224, as said below
- assign: int32 [96], P('rep'), parts along dimension 0, may hold values from 0 to 11, as said below
- out_weight: bfloat16 [5120, 5120], P('tp', 'sec'), may hold values from -0.078125 to 0.078125
- norm_gain: bfloat16 [5120], P('sec'), may hold values from 0.099609375 to 1.8984375
- gate_weight: bfloat16 [5120, 16384], P('sec', 'tp'), may hold values from -0.078125 to 0.078125
- up_weight: bfloat16 [5120, 16384], P('sec', 'tp'), may hold values from -0.078125 to 0.078125
- down_weight: bfloat16 [16384, 5120], P('tp', 'sec'), may hold values from -0.046875 to 0.046875
Outputs:
- layer_out: bfloat16 [96, 5120], P(('rep', 'tp'), 'sec'), parts along dimension 0
There are 2 independent parts, one for each index of `rep`. A program takes and returns all parts, laid end to end along the dimension named above; an argument that names none is the same for every part. Nothing has to cross between parts.
Inputs may be any that keep to these rules, and one draw needn't show every extreme that they name: `assign`: each block of 12 consecutive requests names every slot 0 to 11 exactly once. `cache_len`: some cache slot has all 224 positions valid.
All inputs are finite; a program needn't handle non-finite values.
Results may differ from a plain program's by a relative error of at most 0.025.
Values may be sent and summed in bfloat16 or wider, within the bound.
A program may use at most 64 MiB of HBM per device.

v0:
```python
import functools
import math

import jax
import jax.numpy as jnp
from jax import lax
from jax.experimental import pallas as pl
from jax.experimental.pallas import tpu as pltpu
from jax.sharding import PartitionSpec as P

D = 5120
QUERY_HEADS = 40
KEY_VALUE_HEADS = 8
HEAD_WIDTH = 128
CACHE_SLOTS = 224


def attend_slots(query_rows, key_value_pairs, stored_keys, stored_values, lengths):
    cache_slots = query_rows.shape[0]
    group_query = QUERY_HEADS // KEY_VALUE_HEADS
    query_head_rows = query_rows.reshape(cache_slots, KEY_VALUE_HEADS, group_query, HEAD_WIDTH)
    paired_heads = key_value_pairs.reshape(cache_slots, KEY_VALUE_HEADS, 2, HEAD_WIDTH)
    fresh_keys = paired_heads[:, :, 0]
    fresh_values = paired_heads[:, :, 1]
    earlier_keys = stored_keys.reshape(cache_slots, CACHE_SLOTS, KEY_VALUE_HEADS, HEAD_WIDTH)
    earlier_values = stored_values.reshape(cache_slots, CACHE_SLOTS, KEY_VALUE_HEADS, HEAD_WIDTH)
    scaling = 1.0 / math.sqrt(HEAD_WIDTH)
    past_scores = (
        jnp.einsum(
            "rkgd,rlkd->rkgl", query_head_rows, earlier_keys, preferred_element_type=jnp.float32
        )
        * scaling
    )
    fresh_scores = (
        jnp.einsum("rkgd,rkd->rkg", query_head_rows, fresh_keys, preferred_element_type=jnp.float32)
        * scaling
    )
    valid = lax.broadcasted_iota(jnp.int32, (cache_slots, CACHE_SLOTS), 1) < lengths[:, None]
    past_scores = jnp.where(valid[:, None, None, :], past_scores, -1e30)
    highest = jnp.maximum(jnp.max(past_scores, axis=-1), fresh_scores)
    past_exp = jnp.exp(past_scores - highest[..., None])
    fresh_exp = jnp.exp(fresh_scores - highest)
    denominator = jnp.sum(past_exp, axis=-1) + fresh_exp
    past_weights = (past_exp / denominator[..., None]).astype(jnp.bfloat16)
    fresh_weights = (fresh_exp / denominator).astype(jnp.bfloat16)
    mixed = jnp.einsum(
        "rkgl,rlkd->rkgd", past_weights, earlier_values, preferred_element_type=jnp.float32
    )
    mixed = (
        mixed
        + fresh_weights.astype(jnp.float32)[..., None]
        * fresh_values.astype(jnp.float32)[:, :, None, :]
    )
    return mixed.reshape(cache_slots, QUERY_HEADS * HEAD_WIDTH).astype(jnp.bfloat16)


def gated_units(values, width):
    return (jax.nn.silu(values[:, :width]) * values[:, width:]).astype(jnp.bfloat16)


MESH = pl.DeviceIdType.MESH
ROWS16 = 16


def up_to(count, multiple):
    return -(-count // multiple) * multiple


def fits_kernel(shapes):
    group, per_device, head_cols, width, sec, tp = shapes
    return (
        sec % 2 == 0
        and width % (sec * 256) == 0
        and head_cols % (256) == 0
        and (D // sec) % 256 == 0
        and QUERY_HEADS % tp == 0
        and QUERY_HEADS % sec == 0
        and per_device <= 8
        and per_device * sec == group
        and (group * tp) % 16 == 0
        and group * tp <= 128
    )


def fused_kernel(
    dims,
    resid,
    query,
    new_kv,
    assign,
    gain,
    lengths,
    keys,
    values,
    w_out,
    w_gate,
    w_up,
    w_down,
    out,
    kbuf,
    vbuf,
    wo,
    wg,
    wu,
    wd,
    a_q,
    a_kv,
    a_q_in,
    a_kv_in,
    qheads,
    oheads,
    slot_rows,
    b1,
    b1_in,
    b2_in,
    ord_buf,
    c_out,
    c_in,
    d_in,
    q_in,
    x_buf,
    s_in,
    e_out,
    pair_in,
    e_in,
    f_in,
    acc,
    g_out,
    g_in,
    stream_buf,
    local_sem,
    sec_send,
    sec_recv,
    tp_send,
    tp_recv,
    hop_send,
    hop_recv,
):
    S, T, G, R = dims
    N = G * T
    TR = T * R
    TRP = up_to(TR, ROWS16)
    Dl = resid.shape[1]
    Hl = w_out.shape[0]
    F = w_gate.shape[1]
    Fs = F // S
    f32, bf16 = jnp.float32, jnp.bfloat16
    s = lax.axis_index("sec")
    t = lax.axis_index("tp")
    sx, sc = s // 2, s % 2
    half = S // 2
    steps = [(dx, dc) for dx in list(range(1, half)) + [0] for dc in (0, 1) if dx or dc]
    sec_peers = [((sx + dx) % half) * 2 + (sc + dc) % 2 for dx, dc in steps]
    tp_peers = [(t + k) % T for k in sorted(range(1, T), key=lambda k: -min(k, T - k))]

    barrier = pltpu.get_barrier_semaphore()
    for c in sec_peers:
        pl.semaphore_signal(barrier, inc=1, device_id={"sec": c}, device_id_type=MESH)
    for c in tp_peers:
        pl.semaphore_signal(barrier, inc=1, device_id={"tp": c}, device_id_type=MESH)

    copies = {}
    count = [0]

    def fetch(name, src, dst):
        copy = pltpu.make_async_copy(src, dst, local_sem.at[count[0]])
        count[0] += 1
        copy.start()
        copies[name] = copy

    for r in range(R):
        fetch(("k", r), keys.at[r], kbuf.at[r])
        fetch(("v", r), values.at[r], vbuf.at[r])
    def at_step(dx, dc):
        return ((sx + dx) % half) * 2 + (sc + dc) % 2

    order = [(dx, dc) for dx in list(range(1, half)) + [0] for dc in (1, 0)]

    row_a = assign[...].astype(f32)
    ii = lax.broadcasted_iota(jnp.int32, (N, N), 0)
    jj = lax.broadcasted_iota(jnp.int32, (N, N), 1)
    col_a = jnp.sum(jnp.where(ii == jj, jnp.broadcast_to(row_a, (N, N)), 0.0), axis=1, keepdims=True)
    pi = lax.broadcasted_iota(jnp.int32, (N, G), 0)
    pj = lax.broadcasted_iota(jnp.int32, (N, G), 1)
    own_a = jnp.sum(
        jnp.where(pi == pj + t * G, jnp.broadcast_to(col_a, (N, G)), 0.0), axis=0, keepdims=True
    )
    pr = lax.broadcasted_iota(jnp.int32, (S * 8, 1), 0)
    slot = jnp.full((S * 8, 1), -1.0, f32)
    for c in range(S):
        for r in range(R):
            slot = jnp.where(pr == c * 8 + r, float(c * R + r), slot)
    picker = jnp.where(
        jnp.broadcast_to(slot, (S * 8, G)) == jnp.broadcast_to(own_a, (S * 8, G)), 1.0, 0.0
    ).astype(bf16)
    picked_q = jnp.dot(picker, query[...], preferred_element_type=f32)
    picked_kv = jnp.dot(picker, new_kv[...], preferred_element_type=f32)
    for c in range(S):
        a_q[c] = picked_q[c * 8 : c * 8 + 8].astype(bf16)
        a_kv[c] = picked_kv[c * 8 : c * 8 + 8].astype(bf16)
    pl.semaphore_wait(barrier, len(sec_peers) + len(tp_peers))

    started = []

    def sec_push(phase, i, src, dst):
        copy = pltpu.make_async_remote_copy(
            src_ref=src,
            dst_ref=dst,
            send_sem=sec_send.at[phase, i],
            recv_sem=sec_recv.at[phase, i],
            device_id={"sec": sec_peers[i]},
            device_id_type=MESH,
        )
        copy.start()
        started.append(copy)
        return copy

    def tp_push(phase, i, src, dst):
        copy = pltpu.make_async_remote_copy(
            src_ref=src,
            dst_ref=dst,
            send_sem=tp_send.at[phase, i],
            recv_sem=tp_recv.at[phase, i],
            device_id={"tp": tp_peers[i]},
            device_id_type=MESH,
        )
        copy.start()
        started.append(copy)
        return copy

    SP, TP = len(sec_peers), len(tp_peers)
    pend = []
    for i in range(SP):
        pend.append(sec_push(0, i, a_q.at[sec_peers[i]], a_q_in.at[s]))
        pend.append(sec_push(1, i, a_kv.at[sec_peers[i]], a_kv_in.at[s]))
    a_q_in[s] = a_q[s]
    a_kv_in[s] = a_kv[s]
    oheads[...] = jnp.zeros(oheads.shape, f32)
    slot_rows[...] = jnp.zeros(slot_rows.shape, f32)
    for copy in pend:
        copy.wait_recv()

    fetch("wo", w_out, wo)
    for step in order:
        c = at_step(*step)
        cols = pl.ds(pl.multiple_of(c * Fs, Fs), Fs)
        fetch(("g", step), w_gate.at[:, cols], wg.at[c])
        fetch(("u", step), w_up.at[:, cols], wu.at[c])

    hs = QUERY_HEADS // S
    ht = QUERY_HEADS // T
    HW = HEAD_WIDTH
    GQ = QUERY_HEADS // KEY_VALUE_HEADS
    for c in range(S):
        blk = a_q_in[c].astype(f32)
        for j in range(hs):
            for r in range(R):
                qheads[r, c * hs + j : c * hs + j + 1, :] = blk[r : r + 1, j * HW : (j + 1) * HW]
    pairs = jnp.concatenate([a_kv_in[c].astype(f32) for c in range(S)], axis=1)
    new_k = jnp.concatenate(
        [pairs[:, 2 * k * HW : (2 * k + 1) * HW] for k in range(KEY_VALUE_HEADS)], axis=1
    )
    new_v = jnp.concatenate(
        [pairs[:, (2 * k + 1) * HW : (2 * k + 2) * HW] for k in range(KEY_VALUE_HEADS)], axis=1
    )
    KW = KEY_VALUE_HEADS * HW
    hrow = lax.broadcasted_iota(jnp.int32, (QUERY_HEADS, KW), 0)
    hcol = lax.broadcasted_iota(jnp.int32, (QUERY_HEADS, KW), 1)
    low = jnp.zeros((QUERY_HEADS, KW), jnp.int32)
    for k in range(1, KEY_VALUE_HEADS):
        low = low + jnp.where(hcol >= k * HW, 1, 0)
    diag = (hrow >= low * GQ) & (hrow < low * GQ + GQ)
    scaling = 1.0 / math.sqrt(HW)
    slots = keys.shape[1]
    for r in range(R):
        wide_q = jnp.where(diag, jnp.concatenate([qheads[r]] * KEY_VALUE_HEADS, axis=1), 0.0)
        copies[("k", r)].wait()
        past = (
            lax.dot_general(
                wide_q.astype(bf16),
                kbuf[r],
                (((1,), (1,)), ((), ())),
                preferred_element_type=f32,
            )
            * scaling
        )
        fresh = jnp.sum(wide_q * new_k[r : r + 1, :], axis=1, keepdims=True) * scaling
        valid = lax.broadcasted_iota(jnp.int32, (QUERY_HEADS, slots), 1) < lengths[r]
        past = jnp.where(valid, past, -1e30)
        highest = jnp.maximum(jnp.max(past, axis=1, keepdims=True), fresh)
        past_exp = jnp.exp(past - highest)
        fresh_exp = jnp.exp(fresh - highest)
        denominator = jnp.sum(past_exp, axis=1, keepdims=True) + fresh_exp
        past_w = (past_exp / denominator).astype(bf16)
        fresh_w = (fresh_exp / denominator).astype(bf16).astype(f32)
        copies[("v", r)].wait()
        mixed = jnp.dot(past_w, vbuf[r], preferred_element_type=f32)
        mixed = jnp.where(diag, mixed + fresh_w * new_v[r : r + 1, :], 0.0)
        small = mixed[:, 0:HW]
        for k in range(1, KEY_VALUE_HEADS):
            small = small + mixed[:, k * HW : (k + 1) * HW]
        for c in range(T):
            oheads[c, r * ht : (r + 1) * ht, :] = small[c * ht : (c + 1) * ht, :]
    for c in range(T):
        b1[c] = oheads[c].astype(bf16)
    pend = [tp_push(0, i, b1.at[tp_peers[i]], b1_in.at[t]) for i in range(TP)]
    b1_in[t] = b1[t]
    for step in reversed(order):
        c = at_step(*step)
        rows = pl.ds(pl.multiple_of(c * Fs, Fs), Fs)
        fetch(("d", step), w_down.at[rows, :], wd.at[c])

    def fold(value):
        return jnp.concatenate([value[:, : Dl // 2], value[:, Dl // 2 :]], axis=0).astype(bf16)

    def unfold(value):
        return jnp.concatenate([value[:G], value[G:]], axis=1)

    pos = jnp.zeros((1, N), f32)
    for a in range(G):
        pos = pos + jnp.where(row_a == float(a), float((a // R) * TRP + a % R), 0.0)
    lane = lax.broadcasted_iota(jnp.int32, (1, N), 1)
    for g in range(1, T):
        pos = pos + jnp.where(lane >= g * G, float(R), 0.0)
    pos_col = jnp.sum(jnp.where(ii == jj, pos, 0.0), axis=1, keepdims=True)
    oj = lax.broadcasted_iota(jnp.int32, (N, S * TRP), 1).astype(f32)
    reorder = jnp.where(oj == pos_col, 1.0, 0.0).astype(bf16)
    for copy in pend:
        copy.wait_recv()
    for c in range(T):
        blk = b1_in[c].astype(f32)
        for r in range(R):
            for j in range(ht):
                slot_rows[c * R + r : c * R + r + 1, j * HW : (j + 1) * HW] = blk[
                    r * ht + j : r * ht + j + 1, :
                ]
    b2_in[s] = slot_rows[...].astype(bf16)
    pend = [sec_push(2, i, b2_in.at[s], b2_in.at[s]) for i in range(SP)]
    copies["wo"].wait()
    for copy in pend:
        copy.wait_recv()
    rows = jnp.concatenate([b2_in[c] for c in range(S)], axis=0)
    ord_buf[...] = jnp.dot(reorder, rows, preferred_element_type=f32).astype(bf16)

    def project(i, carry):
        cols = pl.ds(pl.multiple_of(i * 256, 256), 256)
        acc[:, cols] = jnp.dot(ord_buf[...], wo[:, cols], preferred_element_type=f32)
        return carry

    lax.fori_loop(0, Dl // 256, project, 0, unroll=True)
    for g in range(T):
        c_out[g] = fold(acc[g * G : (g + 1) * G, :])
    pend = [tp_push(1, i, c_out.at[tp_peers[i]], c_in.at[t]) for i in range(TP)]
    c_in[t] = c_out[t]
    for copy in pend:
        copy.wait_recv()
    attn = c_in[0].astype(f32)
    for g in range(1, T):
        attn = attn + c_in[g].astype(f32)
    stream = resid[...].astype(f32) + unfold(attn)
    stream_buf[...] = stream
    d_in[t] = fold(stream * gain[...].astype(f32).reshape(1, Dl))
    squares = jnp.sum(stream * stream, axis=1, keepdims=True)
    qi = lax.broadcasted_iota(jnp.int32, (G, 128), 0)
    qj = lax.broadcasted_iota(jnp.int32, (G, 128), 1)
    squares = jnp.where(qj == qi + t * G, squares, 0.0)
    q_in[t] = jnp.broadcast_to(jnp.sum(squares, axis=0, keepdims=True), (8, 128))
    pend = [tp_push(2, i, d_in.at[t], d_in.at[t]) for i in range(TP)]
    pend_q = [tp_push(3, i, q_in.at[t], q_in.at[t]) for i in range(TP)]
    for copy in pend:
        copy.wait_recv()
    for g in range(T):
        acc[g * G : (g + 1) * G, :] = unfold(d_in[g].astype(f32))
    x_buf[...] = acc[...].astype(bf16)

    mate = at_step(0, 1)
    pushed = [0]

    def push(dest, src, dst):
        copy = pltpu.make_async_remote_copy(
            src_ref=src,
            dst_ref=dst,
            send_sem=hop_send.at[pushed[0]],
            recv_sem=hop_recv.at[pushed[0]],
            device_id={"sec": dest},
            device_id_type=MESH,
        )
        pushed[0] += 1
        copy.start()
        started.append(copy)
        return copy

    def widen(step, part):
        c = at_step(*step)
        copies[("gu"[part], step)].wait()
        weight = (wg, wu)[part]

        def tile(j, carry):
            cols = pl.ds(pl.multiple_of(j * 256, 256), 256)
            into = pl.ds(pl.multiple_of(part * Fs + j * 256, 256), 256)
            e_out[c, :, into] = jnp.dot(
                x_buf[...], weight[c, :, cols], preferred_element_type=f32
            ).astype(bf16)
            return carry

        lax.fori_loop(0, Fs // 256, tile, 0, unroll=True)
        return c

    parts = [pl.ds(0, Fs), pl.ds(Fs, Fs)]
    far_sums = []
    for dx in range(1, half):
        fx = (sx + dx) % half
        pair = []
        for part in (0, 1):
            c = widen((dx, 1), part)
            pair.append(push(mate, e_out.at[c, :, parts[part]], pair_in.at[fx, :, parts[part]]))
        for part in (0, 1):
            c = widen((dx, 0), part)
            pair[part].wait_recv()
            e_out[c, :, parts[part]] = (
                e_out[c, :, parts[part]].astype(f32) + pair_in[fx, :, parts[part]].astype(f32)
            ).astype(bf16)
            far_sums.append(push(c, e_out.at[c, :, parts[part]], e_in.at[sx, :, parts[part]]))
    for copy in pend_q:
        copy.wait_recv()
    squares = q_in[0]
    for g in range(1, T):
        squares = squares + q_in[g]
    s_in[s] = squares
    pend_s = [sec_push(4, k, s_in.at[s], s_in.at[s]) for k in range(SP)]
    pair = []
    for part in (0, 1):
        c = widen((0, 1), part)
        pair.append(push(mate, e_out.at[c, :, parts[part]], pair_in.at[sx, :, parts[part]]))
    for part in (0, 1):
        widen((0, 0), part)
    for copy in pend_s:
        copy.wait_recv()
    squares = s_in[0]
    for c in range(1, S):
        squares = squares + s_in[c]
    inverse = lax.rsqrt(squares[0:1, :] / D + 1e-06)
    ni = lax.broadcasted_iota(jnp.int32, (N, 128), 0)
    nj = lax.broadcasted_iota(jnp.int32, (N, 128), 1)
    inverse = jnp.sum(jnp.where(ni == nj, inverse, 0.0), axis=1, keepdims=True)
    for copy in pair + far_sums:
        copy.wait_recv()
    halves = [pl.ds(0, Fs // 2), pl.ds(Fs // 2, Fs // 2)]
    to_mate, from_far = [], {}
    for h in (0, 1):
        for j in range(Fs // 256):
            lo, hi = h * (Fs // 2) + j * 128, h * (Fs // 2) + (j + 1) * 128

            def total(lo, hi):
                value = e_out[s, :, lo:hi].astype(f32) + pair_in[sx, :, lo:hi].astype(f32)
                for dx in range(1, half):
                    value = value + e_in[(sx + dx) % half, :, lo:hi].astype(f32)
                return value * inverse

            gate, upper = total(lo, hi), total(Fs + lo, Fs + hi)
            f_in[s, :, lo:hi] = (gate / (1.0 + jnp.exp(-gate)) * upper).astype(bf16)
        piece = f_in.at[s, :, halves[h]]
        for dx in range(1, half):
            from_far[(half - dx, h)] = push(at_step(dx, 0), piece, piece)
        to_mate.append(push(mate, piece, piece))

    def lower(step, first=False):
        c = at_step(*step)
        copies[("d", step)].wait()

        def tile(j, carry):
            cols = pl.ds(pl.multiple_of(j * 256, 256), 256)
            part = jnp.dot(f_in[c], wd[c, :, cols], preferred_element_type=f32)
            if not first:
                part = part + acc[:, cols]
            acc[:, cols] = part
            return carry

        lax.fori_loop(0, Dl // 256, tile, 0, unroll=True)

    lower((0, 0), True)
    for copy in to_mate:
        copy.wait_recv()
    lower((0, 1))
    for dx in range(1, half):
        relayed = []
        for h in (0, 1):
            from_far[(dx, h)].wait_recv()
            piece = f_in.at[at_step(dx, 0), :, halves[h]]
            relayed.append(push(mate, piece, piece))
        lower((dx, 0))
        for copy in relayed:
            copy.wait_recv()
        lower((dx, 1))
    for g in range(T):
        g_out[g] = fold(acc[g * G : (g + 1) * G, :])
    pend = [tp_push(4, i, g_out.at[tp_peers[i]], g_in.at[t]) for i in range(TP)]
    g_in[t] = g_out[t]
    for copy in pend:
        copy.wait_recv()
    total = stream_buf[...]
    ff = g_in[0].astype(f32)
    for g in range(1, T):
        ff = ff + g_in[g].astype(f32)
    out[...] = (total + unfold(ff)).astype(bf16)
    for copy in started:
        copy.wait_send()


def local(
    resid,
    query,
    new_kv,
    key_cache,
    cached_value_rows,
    cache_len,
    assign,
    out_weight,
    norm_gain,
    gate_weight,
    up_weight,
    down_weight,
):
    group = query.shape[0]
    per_device = key_cache.shape[0]
    tp_index = lax.axis_index("tp")
    sec_index = lax.axis_index("sec")
    tp_count = lax.axis_size("tp")
    local_slots = lax.dynamic_slice_in_dim(assign, tp_index * group, group)
    full_query, full_pairs = (
        lax.all_gather(query, "sec", axis=1, tiled=True),
        lax.all_gather(new_kv, "sec", axis=1, tiled=True),
    )
    wanted = sec_index * per_device + lax.iota(jnp.int32, per_device)
    picker = (local_slots[None, :] == wanted[:, None]).astype(jnp.bfloat16)
    my_query = jnp.dot(picker, full_query, preferred_element_type=jnp.float32).astype(jnp.bfloat16)
    my_pairs = jnp.dot(picker, full_pairs, preferred_element_type=jnp.float32).astype(jnp.bfloat16)
    attended = attend_slots(my_query, my_pairs, key_cache, cached_value_rows, cache_len)
    request_ids = lax.iota(jnp.int32, group * tp_count)
    slot_block = lax.all_gather(attended, "sec", axis=0, tiled=True)
    received = lax.all_to_all(slot_block, "tp", split_axis=1, concat_axis=0, tiled=True)
    position = request_ids // group * group + assign
    ordered = jnp.take(received, position, axis=0)
    block = ordered
    attn_out = lax.psum_scatter(
        jnp.dot(block, out_weight, preferred_element_type=jnp.float32).astype(jnp.bfloat16),
        "tp",
        scatter_dimension=0,
        tiled=True,
    ).astype(jnp.float32)
    stream = resid.astype(jnp.float32) + attn_out
    squares = lax.psum(jnp.sum(stream * stream, axis=1), "sec")
    inverse = lax.rsqrt(squares / D + 1e-06)
    normed = (stream * inverse[:, None] * norm_gain.astype(jnp.float32)[None, :]).astype(
        jnp.bfloat16
    )
    piece = lax.all_gather(normed, "tp", axis=0, tiled=True)
    gate_part = jnp.dot(piece, gate_weight, preferred_element_type=jnp.float32)
    up_part = jnp.dot(piece, up_weight, preferred_element_type=jnp.float32)
    projected = jnp.concatenate([gate_part, up_part], axis=1)
    width = gate_weight.shape[1]
    share = lax.psum_scatter(
        projected.astype(jnp.bfloat16), "sec", scatter_dimension=0, tiled=True
    ).astype(jnp.float32)
    hidden = lax.all_gather(gated_units(share, width), "sec", axis=0, tiled=True)
    block = hidden
    ff_out = lax.psum_scatter(
        jnp.dot(block, down_weight, preferred_element_type=jnp.float32).astype(jnp.bfloat16),
        "tp",
        scatter_dimension=0,
        tiled=True,
    ).astype(jnp.float32)
    return (stream + ff_out).astype(jnp.bfloat16)


def fused(
    resid,
    query,
    new_kv,
    key_cache,
    cached_value_rows,
    cache_len,
    assign,
    out_weight,
    norm_gain,
    gate_weight,
    up_weight,
    down_weight,
):
    S, T = lax.axis_size("sec"), lax.axis_size("tp")
    G, R = query.shape[0], key_cache.shape[0]
    N = G * T
    RH = up_to(R * (QUERY_HEADS // T), ROWS16)
    TRP = up_to(T * R, ROWS16)
    Dl, Hl, F, kvl = resid.shape[1], out_weight.shape[0], gate_weight.shape[1], new_kv.shape[1]
    Fs = F // S
    bf16, f32 = jnp.bfloat16, jnp.float32
    V = pltpu.VMEM
    vm = pl.BlockSpec(memory_space=pltpu.VMEM)
    hbm = pl.BlockSpec(memory_space=pl.ANY)
    scratch = [
        V(key_cache.shape, bf16),
        V(cached_value_rows.shape, bf16),
        V((Hl, Dl), bf16),
        V((S, Dl, Fs), bf16),
        V((S, Dl, Fs), bf16),
        V((S, Fs, Dl), bf16),
        V((S, 8, Dl), bf16),
        V((S, 8, kvl), bf16),
        V((S, 8, Dl), bf16),
        V((S, 8, kvl), bf16),
        V((R, QUERY_HEADS, HEAD_WIDTH), f32),
        V((T, RH, HEAD_WIDTH), f32),
        V((TRP, Hl), f32),
        V((T, RH, HEAD_WIDTH), bf16),
        V((T, RH, HEAD_WIDTH), bf16),
        V((S, TRP, Hl), bf16),
        V((N, Hl), bf16),
        V((T, 2 * G, Dl // 2), bf16),
        V((T, 2 * G, Dl // 2), bf16),
        V((T, 2 * G, Dl // 2), bf16),
        V((T, 8, 128), f32),
        V((N, Dl), bf16),
        V((S, 8, 128), f32),
        V((S, N, 2 * Fs), bf16),
        V((S // 2, N, 2 * Fs), bf16),
        V((S // 2, N, 2 * Fs), bf16),
        V((S, N, Fs), bf16),
        V((N, Dl), f32),
        V((T, 2 * G, Dl // 2), bf16),
        V((T, 2 * G, Dl // 2), bf16),
        V((G, Dl), f32),
        pltpu.SemaphoreType.DMA((2 * R + 1 + 3 * S,)),
        pltpu.SemaphoreType.DMA((6, S - 1)),
        pltpu.SemaphoreType.DMA((6, S - 1)),
        pltpu.SemaphoreType.DMA((5, T - 1)),
        pltpu.SemaphoreType.DMA((5, T - 1)),
        pltpu.SemaphoreType.DMA((5 * S,)),
        pltpu.SemaphoreType.DMA((5 * S,)),
    ]
    return pl.pallas_call(
        functools.partial(fused_kernel, (S, T, G, R)),
        out_shape=jax.ShapeDtypeStruct(resid.shape, bf16),
        in_specs=[vm, vm, vm, vm, vm, pl.BlockSpec(memory_space=pltpu.SMEM)] + [hbm] * 6,
        out_specs=vm,
        scratch_shapes=scratch,
        compiler_params=pltpu.CompilerParams(
            collective_id=0, has_side_effects=True, vmem_limit_bytes=58 * 2**20
        ),
    )(
        resid,
        query,
        new_kv,
        assign.reshape(1, N),
        norm_gain,
        cache_len,
        key_cache,
        cached_value_rows,
        out_weight,
        gate_weight,
        up_weight,
        down_weight,
    )


def layer(*args):
    query, key_cache, out_weight, gate_weight = args[1], args[3], args[7], args[9]
    shapes = (
        query.shape[0],
        key_cache.shape[0],
        out_weight.shape[0],
        gate_weight.shape[1],
        lax.axis_size("sec"),
        lax.axis_size("tp"),
    )
    return fused(*args) if fits_kernel(shapes) else local(*args)


def solution(mesh):
    return jax.shard_map(
        layer,
        mesh=mesh,
        in_specs=(
            P(("rep", "tp"), "sec"),
            P(("rep", "tp"), "sec"),
            P(("rep", "tp"), "sec"),
            P(("rep", "sec", "tp"), None, None),
            P(("rep", "sec", "tp"), None, None),
            P(("rep", "sec", "tp")),
            P("rep"),
            P("tp", "sec"),
            P("sec"),
            P("sec", "tp"),
            P("sec", "tp"),
            P("tp", "sec"),
        ),
        out_specs=P(("rep", "tp"), "sec"),
        check_vma=False,
    )
```

profile of v0, /device:TPU:0, one launch (start us, length us, event | category | flops | bytes accessed | tf_op | source)
XLA Modules:
  0.0 49.5 jit_solution(12924142940547898739)
XLA Ops:
  0.0 48.1 %shard_map.118 = bf16[12,1280]{1,0:T(8,128)(2,1)} custom-call(bf16[12,1280]{1,0:T(8,128)(2,1)} %resid.1, bf16[12,1280]{1,0:T(8,128)(2,1)} %query.1, bf16[12,512]{1,0:T(8,128)(2,1)} %new_kv.1, s32[1,48]{1,0:T(1,128)} %bitcast.1, bf16[1280]{0:T(1024)(128)(2,1)} %gain.1, s32[3]{0:T(128)} %lengths.1, bf16[3,224,1024]{2,1,0:T(8,128)(2,1)} %keys.1, ...), custom_call_target="tpu_custom_call" | custom-call | tf_op jit(solution)/shard_map/pallas_call | solution.py:641
  48.1 1.4 %copy.14 = bf16[12,1280]{1,0:T(8,128)(2,1)} copy(bf16[12,1280]{1,0:T(8,128)(2,1)} %shard_map.118) | data formatting | bytes 61440
where the time goes:
time: 49.8 us; the launch traced here: 49.5 us
  Pallas kernels  48.1 us (97%)
  local copies, waits for them, and re-layouts  1.4 us (3%)
    pallas_call x1, Pallas kernels, fused(): pl.pallas_call(functools.partial(fused_kernel, (S, T, G, R)), out_shape=j...  48.1 us
    unnamed x1, local copies, waits for them, and re-layouts  1.4 us

commit v1 on v0

--- a/solution.py
+++ b/solution.py
@@ -84,12 +84,12 @@
 
 def fused_kernel(
     dims,
-    resid,
-    query,
-    new_kv,
-    assign,
-    gain,
-    lengths,
+    resid_hbm,
+    query_hbm,
+    new_kv_hbm,
+    assign_hbm,
+    gain_hbm,
+    lengths_hbm,
     keys,
     values,
     w_out,
@@ -97,6 +97,12 @@
     w_up,
     w_down,
     out,
+    resid,
+    query,
+    new_kv,
+    assign,
+    gain,
+    lengths,
     kbuf,
     vbuf,
     wo,
@@ -168,6 +174,12 @@
         copy.start()
         copies[name] = copy
 
+    fetch("assign", assign_hbm, assign)
+    fetch("query", query_hbm, query)
+    fetch("new_kv", new_kv_hbm, new_kv)
+    fetch("lengths", lengths_hbm, lengths)
+    fetch("resid", resid_hbm, resid)
+    fetch("gain", gain_hbm, gain)
     for r in range(R):
         fetch(("k", r), keys.at[r], kbuf.at[r])
         fetch(("v", r), values.at[r], vbuf.at[r])
@@ -176,27 +188,73 @@
 
     order = [(dx, dc) for dx in list(range(1, half)) + [0] for dc in (1, 0)]
 
+    hs = QUERY_HEADS // S
+    ht = QUERY_HEADS // T
+    HW = HEAD_WIDTH
+    GQ = QUERY_HEADS // KEY_VALUE_HEADS
+    GP = up_to(G, ROWS16)
+    RQ = a_q.shape[1]
+    copies["assign"].wait()
     row_a = assign[...].astype(f32)
     ii = lax.broadcasted_iota(jnp.int32, (N, N), 0)
     jj = lax.broadcasted_iota(jnp.int32, (N, N), 1)
     col_a = jnp.sum(jnp.where(ii == jj, jnp.broadcast_to(row_a, (N, N)), 0.0), axis=1, keepdims=True)
-    pi = lax.broadcasted_iota(jnp.int32, (N, G), 0)
-    pj = lax.broadcasted_iota(jnp.int32, (N, G), 1)
-    own_a = jnp.sum(
-        jnp.where(pi == pj + t * G, jnp.broadcast_to(col_a, (N, G)), 0.0), axis=0, keepdims=True
-    )
+
+    def own_slots(width):
+        pi = lax.broadcasted_iota(jnp.int32, (N, width), 0)
+        pj = lax.broadcasted_iota(jnp.int32, (N, width), 1)
+        hit = pi == pj + t * G
+        if width > G:
+            stripe = jnp.zeros((N, width), jnp.int32)
+            for j in range(1, width // GP):
+                stripe = stripe + jnp.where(pj >= j * GP, GP, 0)
+            hit = pi == pj - stripe + t * G
+            hit = hit & (pj - stripe < G)
+        return jnp.sum(
+            jnp.where(hit, jnp.broadcast_to(col_a, (N, width)), 0.0)
+            + jnp.where(hit, 1.0, 0.0),
+            axis=0,
+            keepdims=True,
+        ) - 1.0
+
     pr = lax.broadcasted_iota(jnp.int32, (S * 8, 1), 0)
-    slot = jnp.full((S * 8, 1), -1.0, f32)
+    slot = jnp.full((S * 8, 1), -2.0, f32)
     for c in range(S):
         for r in range(R):
             slot = jnp.where(pr == c * 8 + r, float(c * R + r), slot)
     picker = jnp.where(
-        jnp.broadcast_to(slot, (S * 8, G)) == jnp.broadcast_to(own_a, (S * 8, G)), 1.0, 0.0
+        jnp.broadcast_to(slot, (S * 8, G)) == jnp.broadcast_to(own_slots(G), (S * 8, G)), 1.0, 0.0
     ).astype(bf16)
-    picked_q = jnp.dot(picker, query[...], preferred_element_type=f32)
+    qr = lax.broadcasted_iota(jnp.int32, (S * RQ, 1), 0)
+    block = jnp.zeros((S * RQ, 1), jnp.int32)
+    for c in range(1, S):
+        block = block + jnp.where(qr >= c * RQ, 1, 0)
+    place = qr - block * RQ
+    turn = jnp.zeros((S * RQ, 1), jnp.int32)
+    for r in range(1, R):
+        turn = turn + jnp.where(place >= r * hs, 1, 0)
+    qc = lax.broadcasted_iota(jnp.int32, (1, hs * GP), 1)
+    stripe = jnp.zeros((1, hs * GP), jnp.int32)
+    for j in range(1, hs):
+        stripe = stripe + jnp.where(qc >= j * GP, 1, 0)
+    wanted = jnp.where(place < R * hs, block * R + turn, -2).astype(f32)
+    q_picker = jnp.where(
+        (jnp.broadcast_to(wanted, (S * RQ, hs * GP)) == jnp.broadcast_to(own_slots(hs * GP), (S * RQ, hs * GP)))
+        & (jnp.broadcast_to(place - turn * hs, (S * RQ, hs * GP)) == jnp.broadcast_to(stripe, (S * RQ, hs * GP))),
+        1.0,
+        0.0,
+    ).astype(bf16)
+    copies["query"].wait()
+    tall = query[...].astype(f32)
+    if GP > G:
+        tall = jnp.concatenate([tall, jnp.zeros((GP - G, Dl), f32)], axis=0)
+    stacked = jnp.concatenate([tall[:, j * HW : (j + 1) * HW] for j in range(hs)], axis=0).astype(bf16)
+    picked_q = jnp.dot(q_picker, stacked, preferred_element_type=f32).astype(bf16)
+    for c in range(S):
+        a_q[c] = picked_q[c * RQ : (c + 1) * RQ]
+    copies["new_kv"].wait()
     picked_kv = jnp.dot(picker, new_kv[...], preferred_element_type=f32)
     for c in range(S):
-        a_q[c] = picked_q[c * 8 : c * 8 + 8].astype(bf16)
         a_kv[c] = picked_kv[c * 8 : c * 8 + 8].astype(bf16)
     pl.semaphore_wait(barrier, len(sec_peers) + len(tp_peers))
 
@@ -247,15 +305,14 @@
         fetch(("g", step), w_gate.at[:, cols], wg.at[c])
         fetch(("u", step), w_up.at[:, cols], wu.at[c])
 
-    hs = QUERY_HEADS // S
-    ht = QUERY_HEADS // T
-    HW = HEAD_WIDTH
-    GQ = QUERY_HEADS // KEY_VALUE_HEADS
+    copies["lengths"].wait()
+    for r in range(R):
+        copies[("k", r)].wait()
+        copies[("v", r)].wait()
     for c in range(S):
         blk = a_q_in[c].astype(f32)
-        for j in range(hs):
-            for r in range(R):
-                qheads[r, c * hs + j : c * hs + j + 1, :] = blk[r : r + 1, j * HW : (j + 1) * HW]
+        for r in range(R):
+            qheads[r, c * hs : (c + 1) * hs, :] = blk[r * hs : (r + 1) * hs, :]
     pairs = jnp.concatenate([a_kv_in[c].astype(f32) for c in range(S)], axis=1)
     new_k = jnp.concatenate(
         [pairs[:, 2 * k * HW : (2 * k + 1) * HW] for k in range(KEY_VALUE_HEADS)], axis=1
@@ -272,33 +329,37 @@
     diag = (hrow >= low * GQ) & (hrow < low * GQ + GQ)
     scaling = 1.0 / math.sqrt(HW)
     slots = keys.shape[1]
-    for r in range(R):
-        wide_q = jnp.where(diag, jnp.concatenate([qheads[r]] * KEY_VALUE_HEADS, axis=1), 0.0)
-        copies[("k", r)].wait()
-        past = (
-            lax.dot_general(
-                wide_q.astype(bf16),
-                kbuf[r],
-                (((1,), (1,)), ((), ())),
-                preferred_element_type=f32,
-            )
-            * scaling
+    each = range(R)
+    wide_q = [
+        jnp.where(diag, jnp.concatenate([qheads[r]] * KEY_VALUE_HEADS, axis=1), 0.0) for r in each
+    ]
+    past = [
+        lax.dot_general(
+            wide_q[r].astype(bf16),
+            kbuf[r],
+            (((1,), (1,)), ((), ())),
+            preferred_element_type=f32,
         )
-        fresh = jnp.sum(wide_q * new_k[r : r + 1, :], axis=1, keepdims=True) * scaling
-        valid = lax.broadcasted_iota(jnp.int32, (QUERY_HEADS, slots), 1) < lengths[r]
-        past = jnp.where(valid, past, -1e30)
-        highest = jnp.maximum(jnp.max(past, axis=1, keepdims=True), fresh)
-        past_exp = jnp.exp(past - highest)
-        fresh_exp = jnp.exp(fresh - highest)
-        denominator = jnp.sum(past_exp, axis=1, keepdims=True) + fresh_exp
-        past_w = (past_exp / denominator).astype(bf16)
-        fresh_w = (fresh_exp / denominator).astype(bf16).astype(f32)
-        copies[("v", r)].wait()
-        mixed = jnp.dot(past_w, vbuf[r], preferred_element_type=f32)
-        mixed = jnp.where(diag, mixed + fresh_w * new_v[r : r + 1, :], 0.0)
-        small = mixed[:, 0:HW]
+        * scaling
+        for r in each
+    ]
+    fresh = [
+        jnp.sum(wide_q[r] * new_k[r : r + 1, :], axis=1, keepdims=True) * scaling for r in each
+    ]
+    position = lax.broadcasted_iota(jnp.int32, (QUERY_HEADS, slots), 1)
+    past = [jnp.where(position < lengths[r], past[r], -1e30) for r in each]
+    highest = [jnp.maximum(jnp.max(past[r], axis=1, keepdims=True), fresh[r]) for r in each]
+    past_exp = [jnp.exp(past[r] - highest[r]) for r in each]
+    fresh_exp = [jnp.exp(fresh[r] - highest[r]) for r in each]
+    total = [jnp.sum(past_exp[r], axis=1, keepdims=True) + fresh_exp[r] for r in each]
+    past_w = [(past_exp[r] / total[r]).astype(bf16) for r in each]
+    fresh_w = [(fresh_exp[r] / total[r]).astype(bf16).astype(f32) for r in each]
+    mixed = [jnp.dot(past_w[r], vbuf[r], preferred_element_type=f32) for r in each]
+    for r in each:
+        spread = jnp.where(diag, mixed[r] + fresh_w[r] * new_v[r : r + 1, :], 0.0)
+        small = spread[:, 0:HW]
         for k in range(1, KEY_VALUE_HEADS):
-            small = small + mixed[:, k * HW : (k + 1) * HW]
+            small = small + spread[:, k * HW : (k + 1) * HW]
         for c in range(T):
             oheads[c, r * ht : (r + 1) * ht, :] = small[c * ht : (c + 1) * ht, :]
     for c in range(T):
@@ -357,6 +418,8 @@
     attn = c_in[0].astype(f32)
     for g in range(1, T):
         attn = attn + c_in[g].astype(f32)
+    copies["resid"].wait()
+    copies["gain"].wait()
     stream = resid[...].astype(f32) + unfold(attn)
     stream_buf[...] = stream
     d_in[t] = fold(stream * gain[...].astype(f32).reshape(1, Dl))
@@ -591,6 +654,7 @@
     G, R = query.shape[0], key_cache.shape[0]
     N = G * T
     RH = up_to(R * (QUERY_HEADS // T), ROWS16)
+    RQ = up_to(R * (QUERY_HEADS // S), ROWS16)
     TRP = up_to(T * R, ROWS16)
     Dl, Hl, F, kvl = resid.shape[1], out_weight.shape[0], gate_weight.shape[1], new_kv.shape[1]
     Fs = F // S
@@ -599,15 +663,21 @@
     vm = pl.BlockSpec(memory_space=pltpu.VMEM)
     hbm = pl.BlockSpec(memory_space=pl.ANY)
     scratch = [
+        V(resid.shape, bf16),
+        V(query.shape, bf16),
+        V(new_kv.shape, bf16),
+        V((1, N), jnp.int32),
+        V(norm_gain.shape, bf16),
+        pltpu.SMEM(cache_len.shape, jnp.int32),
         V(key_cache.shape, bf16),
         V(cached_value_rows.shape, bf16),
         V((Hl, Dl), bf16),
         V((S, Dl, Fs), bf16),
         V((S, Dl, Fs), bf16),
         V((S, Fs, Dl), bf16),
-        V((S, 8, Dl), bf16),
+        V((S, RQ, HEAD_WIDTH), bf16),
         V((S, 8, kvl), bf16),
-        V((S, 8, Dl), bf16),
+        V((S, RQ, HEAD_WIDTH), bf16),
         V((S, 8, kvl), bf16),
         V((R, QUERY_HEADS, HEAD_WIDTH), f32),
         V((T, RH, HEAD_WIDTH), f32),
@@ -630,7 +700,7 @@
         V((T, 2 * G, Dl // 2), bf16),
         V((T, 2 * G, Dl // 2), bf16),
         V((G, Dl), f32),
-        pltpu.SemaphoreType.DMA((2 * R + 1 + 3 * S,)),
+        pltpu.SemaphoreType.DMA((2 * R + 7 + 3 * S,)),
         pltpu.SemaphoreType.DMA((6, S - 1)),
         pltpu.SemaphoreType.DMA((6, S - 1)),
         pltpu.SemaphoreType.DMA((5, T - 1)),
@@ -640,12 +710,12 @@
     ]
     return pl.pallas_call(
         functools.partial(fused_kernel, (S, T, G, R)),
-        out_shape=jax.ShapeDtypeStruct(resid.shape, bf16),
-        in_specs=[vm, vm, vm, vm, vm, pl.BlockSpec(memory_space=pltpu.SMEM)] + [hbm] * 6,
+        out_shape=pltpu.VMEM(resid.shape, bf16),
+        in_specs=[hbm] * 12,
         out_specs=vm,
         scratch_shapes=scratch,
         compiler_params=pltpu.CompilerParams(
-            collective_id=0, has_side_effects=True, vmem_limit_bytes=58 * 2**20
+            collective_id=0, has_side_effects=True, vmem_limit_bytes=54 * 2**20
         ),
     )(
         resid,

time: 49.8 us -> 46.1 us (0.926)
  Pallas kernels: 48.1 us -> 45.3 us
  local copies, waits for them, and re-layouts: 1.4 us -> 0.62 us
    pallas_call x1, Pallas kernels: 48.1 us -> 45.3 us  [fused(): pl.pallas_call(functools.partial(fused_kernel, (S, T, G, R)), out_shape=p...]
    unnamed x1, local copies, waits for them, and re-layouts: 1.4 us -> 0.62 us
where the time goes in v1:
time: 46.1 us; the launch traced here: 45.9 us
  Pallas kernels  45.3 us (98%)
  local copies, waits for them, and re-layouts  0.62 us (1%)
    pallas_call x1, Pallas kernels, fused(): pl.pallas_call(functools.partial(fused_kernel, (S, T, G, R)), out_shape=p...  45.3 us

profile of v1, /device:TPU:0, one launch (start us, length us, event | category | flops | bytes accessed | tf_op | source)
XLA Modules:
  0.0 45.9 jit_solution(18090611611434208002)
XLA Ops:
  0.0 45.3 %shard_map.118 = bf16[12,1280]{1,0:T(8,128)(2,1)S(1)} custom-call(bf16[12,1280]{1,0:T(8,128)(2,1)} %resid_hbm.1, bf16[12,1280]{1,0:T(8,128)(2,1)} %query_hbm.1, bf16[12,512]{1,0:T(8,128)(2,1)} %new_kv_hbm.1, s32[1,48]{1,0:T(1,128)} %bitcast.1, bf16[1280]{0:T(1024)(128)(2,1)} %gain_hbm.1, s32[3]{0:T(128)} %lengths_hbm.1, bf16[3,224,1024]{2,1,0:T(8,128)(2,1)} %keys.1, ...), custom_call_target="tpu_custom_call" | custom-call | tf_op jit(solution)/shard_map/pallas_call | solution.py:711
  45.3 0.6 %copy.14 = bf16[12,1280]{1,0:T(8,128)(2,1)} copy(bf16[12,1280]{1,0:T(8,128)(2,1)S(1)} %shard_map.118) | data formatting | bytes 61440

commit v2 on v1

--- a/solution.py
+++ b/solution.py
@@ -60,6 +60,7 @@
 
 MESH = pl.DeviceIdType.MESH
 ROWS16 = 16
+HIDDEN_PARTS = 2
 
 
 def up_to(count, multiple):
@@ -70,12 +71,16 @@
     group, per_device, head_cols, width, sec, tp = shapes
     return (
         sec % 2 == 0
+        and sec >= 4
+        and width % (sec * 256 * HIDDEN_PARTS) == 0
         and width % (sec * 256) == 0
         and head_cols % (256) == 0
         and (D // sec) % 256 == 0
+        and D // sec >= 512
         and QUERY_HEADS % tp == 0
         and QUERY_HEADS % sec == 0
         and per_device <= 8
+        and tp >= 2
         and per_device * sec == group
         and (group * tp) % 16 == 0
         and group * tp <= 128
@@ -115,10 +120,9 @@
     a_kv_in,
     qheads,
     oheads,
-    slot_rows,
     b1,
-    b1_in,
     b2_in,
+    pick_buf,
     ord_buf,
     c_out,
     c_in,
@@ -131,23 +135,19 @@
     e_in,
     f_in,
     acc,
+    far_acc,
+    near_acc,
     g_out,
     g_in,
     stream_buf,
     local_sem,
-    sec_send,
-    sec_recv,
-    tp_send,
-    tp_recv,
-    hop_send,
-    hop_recv,
+    send_sem,
+    recv_sem,
 ):
-    S, T, G, R = dims
+    S, T, G, R, NH = dims
     N = G * T
-    TR = T * R
-    TRP = up_to(TR, ROWS16)
+    RH = b1.shape[1]
     Dl = resid.shape[1]
-    Hl = w_out.shape[0]
     F = w_gate.shape[1]
     Fs = F // S
     f32, bf16 = jnp.float32, jnp.bfloat16
@@ -159,11 +159,15 @@
     sec_peers = [((sx + dx) % half) * 2 + (sc + dc) % 2 for dx, dc in steps]
     tp_peers = [(t + k) % T for k in sorted(range(1, T), key=lambda k: -min(k, T - k))]
 
+    twin = sx * 2 + (1 - sc)
     barrier = pltpu.get_barrier_semaphore()
     for c in sec_peers:
         pl.semaphore_signal(barrier, inc=1, device_id={"sec": c}, device_id_type=MESH)
     for c in tp_peers:
         pl.semaphore_signal(barrier, inc=1, device_id={"tp": c}, device_id_type=MESH)
+        pl.semaphore_signal(
+            barrier, inc=1, device_id={"sec": twin, "tp": c}, device_id_type=MESH
+        )
 
     copies = {}
     count = [0]
@@ -256,45 +260,35 @@
     picked_kv = jnp.dot(picker, new_kv[...], preferred_element_type=f32)
     for c in range(S):
         a_kv[c] = picked_kv[c * 8 : c * 8 + 8].astype(bf16)
-    pl.semaphore_wait(barrier, len(sec_peers) + len(tp_peers))
+    pl.semaphore_wait(barrier, len(sec_peers) + 2 * len(tp_peers))
 
     started = []
 
-    def sec_push(phase, i, src, dst):
+    def push(dest, src, dst):
         copy = pltpu.make_async_remote_copy(
             src_ref=src,
             dst_ref=dst,
-            send_sem=sec_send.at[phase, i],
-            recv_sem=sec_recv.at[phase, i],
-            device_id={"sec": sec_peers[i]},
+            send_sem=send_sem.at[len(started)],
+            recv_sem=recv_sem.at[len(started)],
+            device_id=dest,
             device_id_type=MESH,
         )
         copy.start()
         started.append(copy)
         return copy
 
-    def tp_push(phase, i, src, dst):
-        copy = pltpu.make_async_remote_copy(
-            src_ref=src,
-            dst_ref=dst,
-            send_sem=tp_send.at[phase, i],
-            recv_sem=tp_recv.at[phase, i],
-            device_id={"tp": tp_peers[i]},
-            device_id_type=MESH,
-        )
-        copy.start()
-        started.append(copy)
-        return copy
-
-    SP, TP = len(sec_peers), len(tp_peers)
+    def arrived(pending):
+        for copy in pending:
+            copy.wait_recv()
+
     pend = []
-    for i in range(SP):
-        pend.append(sec_push(0, i, a_q.at[sec_peers[i]], a_q_in.at[s]))
-        pend.append(sec_push(1, i, a_kv.at[sec_peers[i]], a_kv_in.at[s]))
+    for c in sec_peers:
+        pend.append(push({"sec": c}, a_q.at[c], a_q_in.at[s]))
+    for c in sec_peers:
+        pend.append(push({"sec": c}, a_kv.at[c], a_kv_in.at[s]))
     a_q_in[s] = a_q[s]
     a_kv_in[s] = a_kv[s]
     oheads[...] = jnp.zeros(oheads.shape, f32)
-    slot_rows[...] = jnp.zeros(slot_rows.shape, f32)
     for copy in pend:
         copy.wait_recv()
 
@@ -364,141 +358,200 @@
             oheads[c, r * ht : (r + 1) * ht, :] = small[c * ht : (c + 1) * ht, :]
     for c in range(T):
         b1[c] = oheads[c].astype(bf16)
-    pend = [tp_push(0, i, b1.at[tp_peers[i]], b1_in.at[t]) for i in range(TP)]
-    b1_in[t] = b1[t]
+    pend = [push({"sec": twin, "tp": c}, b1.at[c], b2_in.at[twin, t]) for c in tp_peers]
+    pend.append(push({"sec": twin}, b1.at[t], b2_in.at[twin, t]))
     for step in reversed(order):
         c = at_step(*step)
         rows = pl.ds(pl.multiple_of(c * Fs, Fs), Fs)
         fetch(("d", step), w_down.at[rows, :], wd.at[c])
 
+    tiles = Dl // 256
+    cut = (tiles + 1) // 2
+    spans = [(0, cut), (cut, tiles)]
+
     def fold(value):
-        return jnp.concatenate([value[:, : Dl // 2], value[:, Dl // 2 :]], axis=0).astype(bf16)
+        return jnp.concatenate(
+            [
+                jnp.concatenate([value[:, i : i + 128], value[:, i + 128 : i + 256]], axis=0)
+                for i in range(0, value.shape[1], 256)
+            ],
+            axis=1,
+        )
 
     def unfold(value):
-        return jnp.concatenate([value[:G], value[G:]], axis=1)
+        rows = value.shape[0] // 2
+        return jnp.concatenate(
+            [
+                part
+                for i in range(0, value.shape[1], 128)
+                for part in (value[:rows, i : i + 128], value[rows:, i : i + 128])
+            ],
+            axis=1,
+        )
+
+    def lanes(span):
+        return slice(span[0] * 128, span[1] * 128)
+
+    copies["resid"].wait()
+    copies["gain"].wait()
+    stream_buf[...] = fold(resid[...].astype(f32))
+    gain_rows = fold(jnp.broadcast_to(gain[...].astype(f32).reshape(1, Dl), (G, Dl)))
 
     pos = jnp.zeros((1, N), f32)
     for a in range(G):
-        pos = pos + jnp.where(row_a == float(a), float((a // R) * TRP + a % R), 0.0)
+        c, r = a // R, a % R
+        held = c + 1 - 2 * (c % 2)
+        pos = pos + jnp.where(row_a == float(a), float(held * T * RH + r * ht), 0.0)
     lane = lax.broadcasted_iota(jnp.int32, (1, N), 1)
     for g in range(1, T):
-        pos = pos + jnp.where(lane >= g * G, float(R), 0.0)
+        pos = pos + jnp.where(lane >= g * G, float(RH), 0.0)
     pos_col = jnp.sum(jnp.where(ii == jj, pos, 0.0), axis=1, keepdims=True)
-    oj = lax.broadcasted_iota(jnp.int32, (N, S * TRP), 1).astype(f32)
-    reorder = jnp.where(oj == pos_col, 1.0, 0.0).astype(bf16)
-    for copy in pend:
-        copy.wait_recv()
-    for c in range(T):
-        blk = b1_in[c].astype(f32)
-        for r in range(R):
-            for j in range(ht):
-                slot_rows[c * R + r : c * R + r + 1, j * HW : (j + 1) * HW] = blk[
-                    r * ht + j : r * ht + j + 1, :
-                ]
-    b2_in[s] = slot_rows[...].astype(bf16)
-    pend = [sec_push(2, i, b2_in.at[s], b2_in.at[s]) for i in range(SP)]
+    spot = lax.broadcasted_iota(jnp.int32, (N, S * T * RH), 1).astype(f32)
+    for j in range(ht):
+        pick_buf[j * N : (j + 1) * N, :] = jnp.where(spot == pos_col + float(j), 1.0, 0.0).astype(bf16)
+    arrived(pend)
+    pend = [push({"sec": c}, b2_in.at[s], b2_in.at[s]) for c in sec_peers]
     copies["wo"].wait()
-    for copy in pend:
-        copy.wait_recv()
-    rows = jnp.concatenate([b2_in[c] for c in range(S)], axis=0)
-    ord_buf[...] = jnp.dot(reorder, rows, preferred_element_type=f32).astype(bf16)
-
-    def project(i, carry):
-        cols = pl.ds(pl.multiple_of(i * 256, 256), 256)
-        acc[:, cols] = jnp.dot(ord_buf[...], wo[:, cols], preferred_element_type=f32)
-        return carry
-
-    lax.fori_loop(0, Dl // 256, project, 0, unroll=True)
-    for g in range(T):
-        c_out[g] = fold(acc[g * G : (g + 1) * G, :])
-    pend = [tp_push(1, i, c_out.at[tp_peers[i]], c_in.at[t]) for i in range(TP)]
-    c_in[t] = c_out[t]
-    for copy in pend:
-        copy.wait_recv()
-    attn = c_in[0].astype(f32)
-    for g in range(1, T):
-        attn = attn + c_in[g].astype(f32)
-    copies["resid"].wait()
-    copies["gain"].wait()
-    stream = resid[...].astype(f32) + unfold(attn)
-    stream_buf[...] = stream
-    d_in[t] = fold(stream * gain[...].astype(f32).reshape(1, Dl))
-    squares = jnp.sum(stream * stream, axis=1, keepdims=True)
+    arrived(pend)
+    rows = jnp.concatenate([b2_in[c, g] for c in range(S) for g in range(T)], axis=0)
+    placed = jnp.dot(pick_buf[...], rows, preferred_element_type=f32).astype(bf16)
+    for j in range(ht):
+        ord_buf[:, j * HW : (j + 1) * HW] = placed[j * N : (j + 1) * N]
+
+    def tp_round(out_buf, in_buf, span):
+        return [
+            push({"tp": g}, out_buf.at[g, :, lanes(span)], in_buf.at[t, :, lanes(span)])
+            for g in tp_peers
+        ]
+
+    def tp_sum(out_buf, in_buf, span):
+        value = out_buf[t, :, lanes(span)].astype(f32)
+        for g in tp_peers:
+            value = value + in_buf[g, :, lanes(span)].astype(f32)
+        return value
+
+    def deal(out_buf, i, value):
+        for g in range(T):
+            out_buf[g, :, i * 128 : (i + 1) * 128] = fold(value[g * G : (g + 1) * G, :]).astype(bf16)
+
+    pend = []
+    for span in spans:
+        for i in range(*span):
+            deal(
+                c_out,
+                i,
+                jnp.dot(ord_buf[...], wo[:, i * 256 : (i + 1) * 256], preferred_element_type=f32),
+            )
+        pend.append(tp_round(c_out, c_in, span))
+    squares = jnp.zeros((G, 1), f32)
+    pend_d = []
+    for span, copies_in in zip(spans, pend):
+        arrived(copies_in)
+        stream = stream_buf[:, lanes(span)] + tp_sum(c_out, c_in, span)
+        stream_buf[:, lanes(span)] = stream
+        d_in[t, :, lanes(span)] = (stream * gain_rows[:, lanes(span)]).astype(bf16)
+        piece = d_in.at[t, :, lanes(span)]
+        pend_d.append([push({"tp": g}, piece, piece) for g in tp_peers])
+        part = jnp.sum(stream * stream, axis=1, keepdims=True)
+        squares = squares + part[:G] + part[G:]
     qi = lax.broadcasted_iota(jnp.int32, (G, 128), 0)
     qj = lax.broadcasted_iota(jnp.int32, (G, 128), 1)
     squares = jnp.where(qj == qi + t * G, squares, 0.0)
     q_in[t] = jnp.broadcast_to(jnp.sum(squares, axis=0, keepdims=True), (8, 128))
-    pend = [tp_push(2, i, d_in.at[t], d_in.at[t]) for i in range(TP)]
-    pend_q = [tp_push(3, i, q_in.at[t], q_in.at[t]) for i in range(TP)]
-    for copy in pend:
-        copy.wait_recv()
-    for g in range(T):
-        acc[g * G : (g + 1) * G, :] = unfold(d_in[g].astype(f32))
-    x_buf[...] = acc[...].astype(bf16)
-
-    mate = at_step(0, 1)
-    pushed = [0]
-
-    def push(dest, src, dst):
-        copy = pltpu.make_async_remote_copy(
-            src_ref=src,
-            dst_ref=dst,
-            send_sem=hop_send.at[pushed[0]],
-            recv_sem=hop_recv.at[pushed[0]],
-            device_id={"sec": dest},
-            device_id_type=MESH,
-        )
-        pushed[0] += 1
-        copy.start()
-        started.append(copy)
-        return copy
-
-    def widen(step, part):
+    pend_q = [push({"tp": g}, q_in.at[t], q_in.at[t]) for g in tp_peers]
+
+    def take(span):
+        for i in range(*span):
+            blks = [d_in[g, :, i * 128 : (i + 1) * 128].astype(f32) for g in range(T)]
+            for side in (0, 1):
+                cols = slice(i * 256 + side * 128, i * 256 + side * 128 + 128)
+                x_buf[:, cols] = jnp.concatenate(
+                    [blk[side * G : side * G + G] for blk in blks], axis=0
+                ).astype(bf16)
+
+    mate = {"sec": at_step(0, 1)}
+    Fh = Fs // NH
+    parts = range(NH)
+    ready = set()
+
+    def need(step):
+        for part in "gu":
+            if (part, step) not in ready:
+                copies[(part, step)].wait()
+                ready.add((part, step))
+
+    def widen(step, h, depth, base=None):
+        need(step)
         c = at_step(*step)
-        copies[("gu"[part], step)].wait()
-        weight = (wg, wu)[part]
-
-        def tile(j, carry):
-            cols = pl.ds(pl.multiple_of(j * 256, 256), 256)
-            into = pl.ds(pl.multiple_of(part * Fs + j * 256, 256), 256)
-            e_out[c, :, into] = jnp.dot(
-                x_buf[...], weight[c, :, cols], preferred_element_type=f32
-            ).astype(bf16)
-            return carry
-
-        lax.fori_loop(0, Fs // 256, tile, 0, unroll=True)
-        return c
-
-    parts = [pl.ds(0, Fs), pl.ds(Fs, Fs)]
-    far_sums = []
-    for dx in range(1, half):
-        fx = (sx + dx) % half
-        pair = []
-        for part in (0, 1):
-            c = widen((dx, 1), part)
-            pair.append(push(mate, e_out.at[c, :, parts[part]], pair_in.at[fx, :, parts[part]]))
-        for part in (0, 1):
-            c = widen((dx, 0), part)
-            pair[part].wait_recv()
-            e_out[c, :, parts[part]] = (
-                e_out[c, :, parts[part]].astype(f32) + pair_in[fx, :, parts[part]].astype(f32)
-            ).astype(bf16)
-            far_sums.append(push(c, e_out.at[c, :, parts[part]], e_in.at[sx, :, parts[part]]))
-    for copy in pend_q:
-        copy.wait_recv()
+        value = [
+            jnp.dot(
+                x_buf[:, depth],
+                weight[c, depth, h * Fh : (h + 1) * Fh],
+                preferred_element_type=f32,
+            )
+            for weight in (wg, wu)
+        ]
+        value = jnp.concatenate(value, axis=1)
+        return value if base is None else base + value
+
+    def unit_cols(h):
+        return slice(h * 2 * Fh, (h + 1) * 2 * Fh)
+
+    first, second = [slice(lo * 256, hi * 256) for lo, hi in spans]
+    whole = slice(0, Dl)
+    far = list(range(1, half))
+    arrived(pend_d[0])
+    take(spans[0])
+    for n, dx in enumerate(far):
+        for dc in (0, 1):
+            for h in parts:
+                far_acc[2 * n + dc, :, unit_cols(h)] = widen((dx, dc), h, first)
+    arrived(pend_d[1])
+    take(spans[1])
+    arrived(pend_q)
     squares = q_in[0]
     for g in range(1, T):
         squares = squares + q_in[g]
     s_in[s] = squares
-    pend_s = [sec_push(4, k, s_in.at[s], s_in.at[s]) for k in range(SP)]
-    pair = []
-    for part in (0, 1):
-        c = widen((0, 1), part)
-        pair.append(push(mate, e_out.at[c, :, parts[part]], pair_in.at[sx, :, parts[part]]))
-    for part in (0, 1):
-        widen((0, 0), part)
-    for copy in pend_s:
-        copy.wait_recv()
+    pend_s = [push({"sec": c}, s_in.at[s], s_in.at[s]) for c in sec_peers]
+    pair, far_sums = {}, {}
+    for n, dx in enumerate(far):
+        fx = (sx + dx) % half
+        c = at_step(dx, 0)
+        for h in parts:
+            e_out[c, :, unit_cols(h)] = widen(
+                (dx, 0), h, second, far_acc[2 * n, :, unit_cols(h)]
+            ).astype(bf16)
+            pair[(dx, h)] = push(
+                mate, e_out.at[c, :, unit_cols(h)], pair_in.at[fx, :, unit_cols(h)]
+            )
+        for h in parts:
+            far_acc[2 * n + 1, :, unit_cols(h)] = widen(
+                (dx, 1), h, second, far_acc[2 * n + 1, :, unit_cols(h)]
+            )
+
+    def near_mate(h):
+        c = at_step(0, 1)
+        e_out[c, :, unit_cols(h)] = widen((0, 1), h, whole).astype(bf16)
+        pair[(0, h)] = push(mate, e_out.at[c, :, unit_cols(h)], pair_in.at[sx, :, unit_cols(h)])
+
+    near_mate(0)
+    for h in parts:
+        for n, dx in enumerate(far):
+            fx = (sx + dx) % half
+            c = at_step(dx, 1)
+            pair[(dx, h)].wait_recv()
+            e_out[c, :, unit_cols(h)] = (
+                far_acc[2 * n + 1, :, unit_cols(h)] + pair_in[fx, :, unit_cols(h)].astype(f32)
+            ).astype(bf16)
+            far_sums[(dx, h)] = push(
+                {"sec": c}, e_out.at[c, :, unit_cols(h)], e_in.at[sx, :, unit_cols(h)]
+            )
+    for h in parts[1:]:
+        near_mate(h)
+    for h in parts:
+        near_acc[:, unit_cols(h)] = widen((0, 0), h, whole)
+    arrived(pend_s)
     squares = s_in[0]
     for c in range(1, S):
         squares = squares + s_in[c]
@@ -506,66 +559,70 @@
     ni = lax.broadcasted_iota(jnp.int32, (N, 128), 0)
     nj = lax.broadcasted_iota(jnp.int32, (N, 128), 1)
     inverse = jnp.sum(jnp.where(ni == nj, inverse, 0.0), axis=1, keepdims=True)
-    for copy in pair + far_sums:
-        copy.wait_recv()
-    halves = [pl.ds(0, Fs // 2), pl.ds(Fs // 2, Fs // 2)]
     to_mate, from_far = [], {}
-    for h in (0, 1):
-        for j in range(Fs // 256):
-            lo, hi = h * (Fs // 2) + j * 128, h * (Fs // 2) + (j + 1) * 128
-
-            def total(lo, hi):
-                value = e_out[s, :, lo:hi].astype(f32) + pair_in[sx, :, lo:hi].astype(f32)
-                for dx in range(1, half):
-                    value = value + e_in[(sx + dx) % half, :, lo:hi].astype(f32)
-                return value * inverse
-
-            gate, upper = total(lo, hi), total(Fs + lo, Fs + hi)
-            f_in[s, :, lo:hi] = (gate / (1.0 + jnp.exp(-gate)) * upper).astype(bf16)
-        piece = f_in.at[s, :, halves[h]]
-        for dx in range(1, half):
-            from_far[(half - dx, h)] = push(at_step(dx, 0), piece, piece)
+    for h in parts:
+        pair[(0, h)].wait_recv()
+        for dx in far:
+            far_sums[(dx, h)].wait_recv()
+        for j in range(0, Fh, 128):
+            both = []
+            for lo in (h * 2 * Fh + j, h * 2 * Fh + Fh + j):
+                value = near_acc[:, lo : lo + 128] + pair_in[sx, :, lo : lo + 128].astype(f32)
+                for dx in far:
+                    value = value + e_in[(sx + dx) % half, :, lo : lo + 128].astype(f32)
+                both.append(value * inverse)
+            gate, upper = both
+            f_in[s, :, h * Fh + j : h * Fh + j + 128] = (
+                gate / (1.0 + jnp.exp(-gate)) * upper
+            ).astype(bf16)
+        piece = f_in.at[s, :, h * Fh : (h + 1) * Fh]
+        for dx in far:
+            from_far[(half - dx, h)] = push({"sec": at_step(dx, 1)}, piece, piece)
         to_mate.append(push(mate, piece, piece))
 
-    def lower(step, first=False):
+    def lower(step, units, first=False):
         c = at_step(*step)
+        for i in range(tiles):
+            cols = slice(i * 256, (i + 1) * 256)
+            value = jnp.dot(f_in[c, :, units], wd[c, units, cols], preferred_element_type=f32)
+            acc[:, cols] = value if first else acc[:, cols] + value
+
+    for step in order:
         copies[("d", step)].wait()
-
-        def tile(j, carry):
-            cols = pl.ds(pl.multiple_of(j * 256, 256), 256)
-            part = jnp.dot(f_in[c], wd[c, :, cols], preferred_element_type=f32)
-            if not first:
-                part = part + acc[:, cols]
-            acc[:, cols] = part
-            return carry
-
-        lax.fori_loop(0, Dl // 256, tile, 0, unroll=True)
-
-    lower((0, 0), True)
-    for copy in to_mate:
-        copy.wait_recv()
-    lower((0, 1))
-    for dx in range(1, half):
-        relayed = []
-        for h in (0, 1):
+    all_units = slice(0, Fs)
+    lower((0, 0), all_units, True)
+    arrived(to_mate)
+    lower((0, 1), all_units)
+    relayed = {}
+    for h in parts:
+        for dx in far:
             from_far[(dx, h)].wait_recv()
-            piece = f_in.at[at_step(dx, 0), :, halves[h]]
-            relayed.append(push(mate, piece, piece))
-        lower((dx, 0))
-        for copy in relayed:
-            copy.wait_recv()
-        lower((dx, 1))
-    for g in range(T):
-        g_out[g] = fold(acc[g * G : (g + 1) * G, :])
-    pend = [tp_push(4, i, g_out.at[tp_peers[i]], g_in.at[t]) for i in range(TP)]
-    g_in[t] = g_out[t]
-    for copy in pend:
-        copy.wait_recv()
-    total = stream_buf[...]
-    ff = g_in[0].astype(f32)
-    for g in range(1, T):
-        ff = ff + g_in[g].astype(f32)
-    out[...] = (total + unfold(ff)).astype(bf16)
+            piece = f_in.at[at_step(dx, 1), :, h * Fh : (h + 1) * Fh]
+            relayed[(dx, h)] = push(mate, piece, piece)
+    for dx in far:
+        lower((dx, 1), all_units)
+    early = slice(0, (NH - 1) * Fh)
+    late = slice((NH - 1) * Fh, Fs)
+    for dx in far:
+        for h in parts[:-1]:
+            relayed[(dx, h)].wait_recv()
+        lower((dx, 0), early)
+    for dx in far[:-1]:
+        relayed[(dx, NH - 1)].wait_recv()
+        lower((dx, 0), late)
+    relayed[(far[-1], NH - 1)].wait_recv()
+    c = at_step(far[-1], 0)
+    pend = []
+    for span in spans:
+        for i in range(*span):
+            cols = slice(i * 256, (i + 1) * 256)
+            value = jnp.dot(f_in[c, :, late], wd[c, late, cols], preferred_element_type=f32)
+            deal(g_out, i, acc[:, cols] + value)
+        pend.append(tp_round(g_out, g_in, span))
+    for span, copies_in in zip(spans, pend):
+        arrived(copies_in)
+        total = stream_buf[:, lanes(span)] + tp_sum(g_out, g_in, span)
+        out[:, span[0] * 256 : span[1] * 256] = unfold(total).astype(bf16)
     for copy in started:
         copy.wait_send()
 
@@ -655,9 +712,10 @@
     N = G * T
     RH = up_to(R * (QUERY_HEADS // T), ROWS16)
     RQ = up_to(R * (QUERY_HEADS // S), ROWS16)
-    TRP = up_to(T * R, ROWS16)
     Dl, Hl, F, kvl = resid.shape[1], out_weight.shape[0], gate_weight.shape[1], new_kv.shape[1]
     Fs = F // S
+    NH = HIDDEN_PARTS
+    remote = 4 * (S - 1) + 10 * (T - 1) + (3 * S // 2 + 2) * NH
     bf16, f32 = jnp.bfloat16, jnp.float32
     V = pltpu.VMEM
     vm = pl.BlockSpec(memory_space=pltpu.VMEM)
@@ -681,10 +739,9 @@
         V((S, 8, kvl), bf16),
         V((R, QUERY_HEADS, HEAD_WIDTH), f32),
         V((T, RH, HEAD_WIDTH), f32),
-        V((TRP, Hl), f32),
         V((T, RH, HEAD_WIDTH), bf16),
-        V((T, RH, HEAD_WIDTH), bf16),
-        V((S, TRP, Hl), bf16),
+        V((S, T, RH, HEAD_WIDTH), bf16),
+        V((QUERY_HEADS // T * N, S * T * RH), bf16),
         V((N, Hl), bf16),
         V((T, 2 * G, Dl // 2), bf16),
         V((T, 2 * G, Dl // 2), bf16),
@@ -697,19 +754,17 @@
         V((S // 2, N, 2 * Fs), bf16),
         V((S, N, Fs), bf16),
         V((N, Dl), f32),
+        V((2 * (S // 2 - 1), N, 2 * Fs), f32),
+        V((N, 2 * Fs), f32),
         V((T, 2 * G, Dl // 2), bf16),
         V((T, 2 * G, Dl // 2), bf16),
-        V((G, Dl), f32),
+        V((2 * G, Dl // 2), f32),
         pltpu.SemaphoreType.DMA((2 * R + 7 + 3 * S,)),
-        pltpu.SemaphoreType.DMA((6, S - 1)),
-        pltpu.SemaphoreType.DMA((6, S - 1)),
-        pltpu.SemaphoreType.DMA((5, T - 1)),
-        pltpu.SemaphoreType.DMA((5, T - 1)),
-        pltpu.SemaphoreType.DMA((5 * S,)),
-        pltpu.SemaphoreType.DMA((5 * S,)),
+        pltpu.SemaphoreType.DMA((remote,)),
+        pltpu.SemaphoreType.DMA((remote,)),
     ]
     return pl.pallas_call(
-        functools.partial(fused_kernel, (S, T, G, R)),
+        functools.partial(fused_kernel, (S, T, G, R, NH)),
         out_shape=pltpu.VMEM(resid.shape, bf16),
         in_specs=[hbm] * 12,
         out_specs=vm,

time: 46.1 us -> 44.4 us (0.963)
  Pallas kernels: 45.3 us -> 43.6 us
    pallas_call x1, Pallas kernels: 45.3 us -> 43.6 us  [fused(): pl.pallas_call(functools.partial(fused_kernel, (S, T, G, R, NH)), out_sha...]
where the time goes in v2:
time: 44.4 us; the launch traced here: 44.2 us
  Pallas kernels  43.6 us (98%)
  local copies, waits for them, and re-layouts  0.62 us (1%)
    pallas_call x1, Pallas kernels, fused(): pl.pallas_call(functools.partial(fused_kernel, (S, T, G, R, NH)), out_sha...  43.6 us

profile of v2, /device:TPU:0, one launch (start us, length us, event | category | flops | bytes accessed | tf_op | source)
XLA Modules:
  0.0 44.2 jit_solution(1754373197667803743)
XLA Ops:
  0.0 43.6 %shard_map.118 = bf16[12,1280]{1,0:T(8,128)(2,1)S(1)} custom-call(bf16[12,1280]{1,0:T(8,128)(2,1)} %resid_hbm.1, bf16[12,1280]{1,0:T(8,128)(2,1)} %query_hbm.1, bf16[12,512]{1,0:T(8,128)(2,1)} %new_kv_hbm.1, s32[1,48]{1,0:T(1,128)} %bitcast.1, bf16[1280]{0:T(1024)(128)(2,1)} %gain_hbm.1, s32[3]{0:T(128)} %lengths_hbm.1, bf16[3,224,1024]{2,1,0:T(8,128)(2,1)} %keys.1, ...), custom_call_target="tpu_custom_call" | custom-call | tf_op jit(solution)/shard_map/pallas_call | solution.py:766
  43.6 0.6 %copy.14 = bf16[12,1280]{1,0:T(8,128)(2,1)} copy(bf16[12,1280]{1,0:T(8,128)(2,1)S(1)} %shard_map.118) | data formatting | bytes 61440

commit v3 on v2

--- a/solution.py
+++ b/solution.py
@@ -158,6 +158,8 @@
     steps = [(dx, dc) for dx in list(range(1, half)) + [0] for dc in (0, 1) if dx or dc]
     sec_peers = [((sx + dx) % half) * 2 + (sc + dc) % 2 for dx, dc in steps]
     tp_peers = [(t + k) % T for k in sorted(range(1, T), key=lambda k: -min(k, T - k))]
+    if T == 4:
+        tp_peers = [T - 1 - t, (t + 2) % T, t + 1 - 2 * (t % 2)]
 
     twin = sx * 2 + (1 - sc)
     barrier = pltpu.get_barrier_semaphore()

time: 44.4 us -> 44 us (level)
  no operation moved by 1% of the time
where the time goes in v3:
time: 44 us; the launch traced here: 43.8 us
  Pallas kernels  43.2 us (98%)
  local copies, waits for them, and re-layouts  0.62 us (1%)
    pallas_call x1, Pallas kernels, fused(): pl.pallas_call(functools.partial(fused_kernel, (S, T, G, R, NH)), out_sha...  43.2 us

profile of v3, /device:TPU:0, one launch (start us, length us, event | category | flops | bytes accessed | tf_op | source)
XLA Modules:
  0.0 43.8 jit_solution(2080342298963986790)
XLA Ops:
  0.0 43.2 %shard_map.118 = bf16[12,1280]{1,0:T(8,128)(2,1)S(1)} custom-call(bf16[12,1280]{1,0:T(8,128)(2,1)} %resid_hbm.1, bf16[12,1280]{1,0:T(8,128)(2,1)} %query_hbm.1, bf16[12,512]{1,0:T(8,128)(2,1)} %new_kv_hbm.1, s32[1,48]{1,0:T(1,128)} %bitcast.1, bf16[1280]{0:T(1024)(128)(2,1)} %gain_hbm.1, s32[3]{0:T(128)} %lengths_hbm.1, bf16[3,224,1024]{2,1,0:T(8,128)(2,1)} %keys.1, ...), custom_call_target="tpu_custom_call" | custom-call | tf_op jit(solution)/shard_map/pallas_call | solution.py:768
  43.2 0.6 %copy.14 = bf16[12,1280]{1,0:T(8,128)(2,1)} copy(bf16[12,1280]{1,0:T(8,128)(2,1)S(1)} %shard_map.118) | data formatting | bytes 61440

commit v4 on v3

--- a/solution.py
+++ b/solution.py
@@ -61,6 +61,7 @@
 MESH = pl.DeviceIdType.MESH
 ROWS16 = 16
 HIDDEN_PARTS = 2
+SENDS = 16
 
 
 def up_to(count, multiple):
@@ -172,11 +173,16 @@
         )
 
     copies = {}
-    count = [0]
-
-    def fetch(name, src, dst):
-        copy = pltpu.make_async_copy(src, dst, local_sem.at[count[0]])
-        count[0] += 1
+    count, used = [0], {}
+
+    def fetch(name, src, dst, after=None):
+        if after is None:
+            slot = count[0]
+            count[0] += 1
+        else:
+            slot = used[after]
+        used[name] = slot
+        copy = pltpu.make_async_copy(src, dst, local_sem.at[slot])
         copy.start()
         copies[name] = copy
 
@@ -266,12 +272,31 @@
 
     started = []
 
-    def push(dest, src, dst):
+    sends = send_sem.shape[0]
+    taken = [0]
+
+    def fresh(amount):
+        taken[0] += amount
+        return list(range(taken[0] - amount, taken[0]))
+
+    query_slots, kv_slots = fresh(S - 1), fresh(S - 1)
+    head_slots, gather_slots = fresh(T), fresh(S - 1)
+    sum_slots = fresh(2 * (T - 1))
+    spread_slots = kv_slots + head_slots + gather_slots
+    spread_slots = spread_slots + fresh(max(0, 3 * (T - 1) - len(spread_slots)))
+    list_query, list_kv, list_head = list(query_slots), list(kv_slots), list(head_slots)
+    list_gather, list_sum = list(gather_slots), list(sum_slots)
+    hop_slots = fresh(NH * (4 * (half - 1) + 2))
+
+    def push(dest, src, dst, slots):
+        turn = len(started)
+        if turn >= sends:
+            started[turn - sends].wait_send()
         copy = pltpu.make_async_remote_copy(
             src_ref=src,
             dst_ref=dst,
-            send_sem=send_sem.at[len(started)],
-            recv_sem=recv_sem.at[len(started)],
+            send_sem=send_sem.at[turn % sends],
+            recv_sem=recv_sem.at[slots.pop(0)],
             device_id=dest,
             device_id_type=MESH,
         )
@@ -285,16 +310,16 @@
 
     pend = []
     for c in sec_peers:
-        pend.append(push({"sec": c}, a_q.at[c], a_q_in.at[s]))
+        pend.append(push({"sec": c}, a_q.at[c], a_q_in.at[s], list_query))
     for c in sec_peers:
-        pend.append(push({"sec": c}, a_kv.at[c], a_kv_in.at[s]))
+        pend.append(push({"sec": c}, a_kv.at[c], a_kv_in.at[s], list_kv))
     a_q_in[s] = a_q[s]
     a_kv_in[s] = a_kv[s]
     oheads[...] = jnp.zeros(oheads.shape, f32)
     for copy in pend:
         copy.wait_recv()
 
-    fetch("wo", w_out, wo)
+    fetch("wo", w_out, wo, "assign")
     for step in order:
         c = at_step(*step)
         cols = pl.ds(pl.multiple_of(c * Fs, Fs), Fs)
@@ -360,12 +385,13 @@
             oheads[c, r * ht : (r + 1) * ht, :] = small[c * ht : (c + 1) * ht, :]
     for c in range(T):
         b1[c] = oheads[c].astype(bf16)
-    pend = [push({"sec": twin, "tp": c}, b1.at[c], b2_in.at[twin, t]) for c in tp_peers]
-    pend.append(push({"sec": twin}, b1.at[t], b2_in.at[twin, t]))
+    pend = [push({"sec": twin, "tp": c}, b1.at[c], b2_in.at[twin, t], list_head) for c in tp_peers]
+    pend.append(push({"sec": twin}, b1.at[t], b2_in.at[twin, t], list_head))
+    spare = [(part, r) for part in "kv" for r in range(R)]
     for step in reversed(order):
         c = at_step(*step)
         rows = pl.ds(pl.multiple_of(c * Fs, Fs), Fs)
-        fetch(("d", step), w_down.at[rows, :], wd.at[c])
+        fetch(("d", step), w_down.at[rows, :], wd.at[c], spare.pop(0) if spare else None)
 
     tiles = Dl // 256
     cut = (tiles + 1) // 2
@@ -412,7 +438,7 @@
     for j in range(ht):
         pick_buf[j * N : (j + 1) * N, :] = jnp.where(spot == pos_col + float(j), 1.0, 0.0).astype(bf16)
     arrived(pend)
-    pend = [push({"sec": c}, b2_in.at[s], b2_in.at[s]) for c in sec_peers]
+    pend = [push({"sec": c}, b2_in.at[s], b2_in.at[s], list_gather) for c in sec_peers]
     copies["wo"].wait()
     arrived(pend)
     rows = jnp.concatenate([b2_in[c, g] for c in range(S) for g in range(T)], axis=0)
@@ -420,9 +446,9 @@
     for j in range(ht):
         ord_buf[:, j * HW : (j + 1) * HW] = placed[j * N : (j + 1) * N]
 
-    def tp_round(out_buf, in_buf, span):
+    def tp_round(out_buf, in_buf, span, slots):
         return [
-            push({"tp": g}, out_buf.at[g, :, lanes(span)], in_buf.at[t, :, lanes(span)])
+            push({"tp": g}, out_buf.at[g, :, lanes(span)], in_buf.at[t, :, lanes(span)], slots)
             for g in tp_peers
         ]
 
@@ -444,7 +470,7 @@
                 i,
                 jnp.dot(ord_buf[...], wo[:, i * 256 : (i + 1) * 256], preferred_element_type=f32),
             )
-        pend.append(tp_round(c_out, c_in, span))
+        pend.append(tp_round(c_out, c_in, span, list_sum))
     squares = jnp.zeros((G, 1), f32)
     pend_d = []
     for span, copies_in in zip(spans, pend):
@@ -453,14 +479,14 @@
         stream_buf[:, lanes(span)] = stream
         d_in[t, :, lanes(span)] = (stream * gain_rows[:, lanes(span)]).astype(bf16)
         piece = d_in.at[t, :, lanes(span)]
-        pend_d.append([push({"tp": g}, piece, piece) for g in tp_peers])
+        pend_d.append([push({"tp": g}, piece, piece, spread_slots) for g in tp_peers])
         part = jnp.sum(stream * stream, axis=1, keepdims=True)
         squares = squares + part[:G] + part[G:]
     qi = lax.broadcasted_iota(jnp.int32, (G, 128), 0)
     qj = lax.broadcasted_iota(jnp.int32, (G, 128), 1)
     squares = jnp.where(qj == qi + t * G, squares, 0.0)
     q_in[t] = jnp.broadcast_to(jnp.sum(squares, axis=0, keepdims=True), (8, 128))
-    pend_q = [push({"tp": g}, q_in.at[t], q_in.at[t]) for g in tp_peers]
+    pend_q = [push({"tp": g}, q_in.at[t], q_in.at[t], spread_slots) for g in tp_peers]
 
     def take(span):
         for i in range(*span):
@@ -515,7 +541,7 @@
     for g in range(1, T):
         squares = squares + q_in[g]
     s_in[s] = squares
-    pend_s = [push({"sec": c}, s_in.at[s], s_in.at[s]) for c in sec_peers]
+    pend_s = [push({"sec": c}, s_in.at[s], s_in.at[s], query_slots) for c in sec_peers]
     pair, far_sums = {}, {}
     for n, dx in enumerate(far):
         fx = (sx + dx) % half
@@ -525,7 +551,7 @@
                 (dx, 0), h, second, far_acc[2 * n, :, unit_cols(h)]
             ).astype(bf16)
             pair[(dx, h)] = push(
-                mate, e_out.at[c, :, unit_cols(h)], pair_in.at[fx, :, unit_cols(h)]
+                mate, e_out.at[c, :, unit_cols(h)], pair_in.at[fx, :, unit_cols(h)], hop_slots
             )
         for h in parts:
             far_acc[2 * n + 1, :, unit_cols(h)] = widen(
@@ -535,7 +561,7 @@
     def near_mate(h):
         c = at_step(0, 1)
         e_out[c, :, unit_cols(h)] = widen((0, 1), h, whole).astype(bf16)
-        pair[(0, h)] = push(mate, e_out.at[c, :, unit_cols(h)], pair_in.at[sx, :, unit_cols(h)])
+        pair[(0, h)] = push(mate, e_out.at[c, :, unit_cols(h)], pair_in.at[sx, :, unit_cols(h)], hop_slots)
 
     near_mate(0)
     for h in parts:
@@ -547,7 +573,7 @@
                 far_acc[2 * n + 1, :, unit_cols(h)] + pair_in[fx, :, unit_cols(h)].astype(f32)
             ).astype(bf16)
             far_sums[(dx, h)] = push(
-                {"sec": c}, e_out.at[c, :, unit_cols(h)], e_in.at[sx, :, unit_cols(h)]
+                {"sec": c}, e_out.at[c, :, unit_cols(h)], e_in.at[sx, :, unit_cols(h)], hop_slots
             )
     for h in parts[1:]:
         near_mate(h)
@@ -579,8 +605,8 @@
             ).astype(bf16)
         piece = f_in.at[s, :, h * Fh : (h + 1) * Fh]
         for dx in far:
-            from_far[(half - dx, h)] = push({"sec": at_step(dx, 1)}, piece, piece)
-        to_mate.append(push(mate, piece, piece))
+            from_far[(half - dx, h)] = push({"sec": at_step(dx, 1)}, piece, piece, hop_slots)
+        to_mate.append(push(mate, piece, piece, hop_slots))
 
     def lower(step, units, first=False):
         c = at_step(*step)
@@ -600,7 +626,7 @@
         for dx in far:
             from_far[(dx, h)].wait_recv()
             piece = f_in.at[at_step(dx, 1), :, h * Fh : (h + 1) * Fh]
-            relayed[(dx, h)] = push(mate, piece, piece)
+            relayed[(dx, h)] = push(mate, piece, piece, hop_slots)
     for dx in far:
         lower((dx, 1), all_units)
     early = slice(0, (NH - 1) * Fh)
@@ -620,12 +646,12 @@
             cols = slice(i * 256, (i + 1) * 256)
             value = jnp.dot(f_in[c, :, late], wd[c, late, cols], preferred_element_type=f32)
             deal(g_out, i, acc[:, cols] + value)
-        pend.append(tp_round(g_out, g_in, span))
+        pend.append(tp_round(g_out, g_in, span, sum_slots))
     for span, copies_in in zip(spans, pend):
         arrived(copies_in)
         total = stream_buf[:, lanes(span)] + tp_sum(g_out, g_in, span)
         out[:, span[0] * 256 : span[1] * 256] = unfold(total).astype(bf16)
-    for copy in started:
+    for copy in started[-sends:]:
         copy.wait_send()
 
 
@@ -717,7 +743,8 @@
     Dl, Hl, F, kvl = resid.shape[1], out_weight.shape[0], gate_weight.shape[1], new_kv.shape[1]
     Fs = F // S
     NH = HIDDEN_PARTS
-    remote = 4 * (S - 1) + 10 * (T - 1) + (3 * S // 2 + 2) * NH
+    landed = 4 * (S - 1) - (S - 1) + T + 2 * (T - 1) + NH * (2 * S - 2)
+    landed = landed + max(0, 3 * (T - 1) - 2 * (S - 1) - T)
     bf16, f32 = jnp.bfloat16, jnp.float32
     V = pltpu.VMEM
     vm = pl.BlockSpec(memory_space=pltpu.VMEM)
@@ -761,9 +788,9 @@
         V((T, 2 * G, Dl // 2), bf16),
         V((T, 2 * G, Dl // 2), bf16),
         V((2 * G, Dl // 2), f32),
-        pltpu.SemaphoreType.DMA((2 * R + 7 + 3 * S,)),
-        pltpu.SemaphoreType.DMA((remote,)),
-        pltpu.SemaphoreType.DMA((remote,)),
+        pltpu.SemaphoreType.DMA((2 * R + 6 + 2 * S + max(0, S - 2 * R),)),
+        pltpu.SemaphoreType.DMA((SENDS,)),
+        pltpu.SemaphoreType.DMA((landed,)),
     ]
     return pl.pallas_call(
         functools.partial(fused_kernel, (S, T, G, R, NH)),

time: 44 us -> 43.3 us (0.984)
  Pallas kernels: 43.2 us -> 42.5 us
    pallas_call x1, Pallas kernels: 43.2 us -> 42.5 us  [fused(): pl.pallas_call(functools.partial(fused_kernel, (S, T, G, R, NH)), out_sha...]
where the time goes in v4:
time: 43.3 us; the launch traced here: 43.1 us
  Pallas kernels  42.5 us (98%)
  local copies, waits for them, and re-layouts  0.62 us (1%)
    pallas_call x1, Pallas kernels, fused(): pl.pallas_call(functools.partial(fused_kernel, (S, T, G, R, NH)), out_sha...  42.5 us

profile of v4, /device:TPU:0, one launch (start us, length us, event | category | flops | bytes accessed | tf_op | source)
XLA Modules:
  0.0 43.1 jit_solution(16968684282396394801)
XLA Ops:
  0.0 42.5 %shard_map.118 = bf16[12,1280]{1,0:T(8,128)(2,1)S(1)} custom-call(bf16[12,1280]{1,0:T(8,128)(2,1)} %resid_hbm.1, bf16[12,1280]{1,0:T(8,128)(2,1)} %query_hbm.1, bf16[12,512]{1,0:T(8,128)(2,1)} %new_kv_hbm.1, s32[1,48]{1,0:T(1,128)} %bitcast.1, bf16[1280]{0:T(1024)(128)(2,1)} %gain_hbm.1, s32[3]{0:T(128)} %lengths_hbm.1, bf16[3,224,1024]{2,1,0:T(8,128)(2,1)} %keys.1, ...), custom_call_target="tpu_custom_call" | custom-call | tf_op jit(solution)/shard_map/pallas_call | solution.py:795
  42.5 0.6 %copy.14 = bf16[12,1280]{1,0:T(8,128)(2,1)} copy(bf16[12,1280]{1,0:T(8,128)(2,1)S(1)} %shard_map.118) | data formatting | bytes 61440

commit v5 on v4

--- a/solution.py
+++ b/solution.py
@@ -60,8 +60,8 @@
 
 MESH = pl.DeviceIdType.MESH
 ROWS16 = 16
-HIDDEN_PARTS = 2
-SENDS = 16
+HIDDEN_PARTS = 4
+SENDS = 10
 
 
 def up_to(count, multiple):
@@ -286,7 +286,9 @@
     spread_slots = spread_slots + fresh(max(0, 3 * (T - 1) - len(spread_slots)))
     list_query, list_kv, list_head = list(query_slots), list(kv_slots), list(head_slots)
     list_gather, list_sum = list(gather_slots), list(sum_slots)
-    hop_slots = fresh(NH * (4 * (half - 1) + 2))
+    hops = NH * (2 * half - 1)
+    hop_slots = fresh(hops)
+    unit_slots = list(spread_slots) + fresh(max(0, hops - len(spread_slots)))
 
     def push(dest, src, dst, slots):
         turn = len(started)
@@ -323,8 +325,9 @@
     for step in order:
         c = at_step(*step)
         cols = pl.ds(pl.multiple_of(c * Fs, Fs), Fs)
-        fetch(("g", step), w_gate.at[:, cols], wg.at[c])
-        fetch(("u", step), w_up.at[:, cols], wu.at[c])
+        first = step == order[0]
+        fetch(("g", step), w_gate.at[:, cols], wg.at[c], "query" if first else None)
+        fetch(("u", step), w_up.at[:, cols], wu.at[c], "new_kv" if first else None)
 
     copies["lengths"].wait()
     for r in range(R):
@@ -605,8 +608,8 @@
             ).astype(bf16)
         piece = f_in.at[s, :, h * Fh : (h + 1) * Fh]
         for dx in far:
-            from_far[(half - dx, h)] = push({"sec": at_step(dx, 1)}, piece, piece, hop_slots)
-        to_mate.append(push(mate, piece, piece, hop_slots))
+            from_far[(half - dx, h)] = push({"sec": at_step(dx, 1)}, piece, piece, unit_slots)
+        to_mate.append(push(mate, piece, piece, unit_slots))
 
     def lower(step, units, first=False):
         c = at_step(*step)
@@ -626,7 +629,7 @@
         for dx in far:
             from_far[(dx, h)].wait_recv()
             piece = f_in.at[at_step(dx, 1), :, h * Fh : (h + 1) * Fh]
-            relayed[(dx, h)] = push(mate, piece, piece, hop_slots)
+            relayed[(dx, h)] = push(mate, piece, piece, unit_slots)
     for dx in far:
         lower((dx, 1), all_units)
     early = slice(0, (NH - 1) * Fh)
@@ -743,8 +746,9 @@
     Dl, Hl, F, kvl = resid.shape[1], out_weight.shape[0], gate_weight.shape[1], new_kv.shape[1]
     Fs = F // S
     NH = HIDDEN_PARTS
-    landed = 4 * (S - 1) - (S - 1) + T + 2 * (T - 1) + NH * (2 * S - 2)
-    landed = landed + max(0, 3 * (T - 1) - 2 * (S - 1) - T)
+    landed = 4 * (S - 1) - (S - 1) + T + 2 * (T - 1) + NH * (S - 1)
+    spread = max(3 * (T - 1), 2 * (S - 1) + T)
+    landed = landed + spread - 2 * (S - 1) - T + max(0, NH * (S - 1) - spread)
     bf16, f32 = jnp.bfloat16, jnp.float32
     V = pltpu.VMEM
     vm = pl.BlockSpec(memory_space=pltpu.VMEM)
@@ -788,7 +792,7 @@
         V((T, 2 * G, Dl // 2), bf16),
         V((T, 2 * G, Dl // 2), bf16),
         V((2 * G, Dl // 2), f32),
-        pltpu.SemaphoreType.DMA((2 * R + 6 + 2 * S + max(0, S - 2 * R),)),
+        pltpu.SemaphoreType.DMA((2 * R + 4 + 2 * S + max(0, S - 2 * R),)),
         pltpu.SemaphoreType.DMA((SENDS,)),
         pltpu.SemaphoreType.DMA((landed,)),
     ]

time: 43.3 us -> 42.8 us (0.988)
  Pallas kernels: 42.5 us -> 42 us
    pallas_call x1, Pallas kernels: 42.5 us -> 42 us  [fused(): pl.pallas_call(functools.partial(fused_kernel, (S, T, G, R, NH)), out_sha...]
where the time goes in v5:
time: 42.8 us; the launch traced here: 42.7 us
  Pallas kernels  42 us (98%)
  local copies, waits for them, and re-layouts  0.62 us (1%)
    pallas_call x1, Pallas kernels, fused(): pl.pallas_call(functools.partial(fused_kernel, (S, T, G, R, NH)), out_sha...  42 us

profile of v5, /device:TPU:0, one launch (start us, length us, event | category | flops | bytes accessed | tf_op | source)
XLA Modules:
  0.0 42.7 jit_solution(7527877829147772477)
XLA Ops:
  0.0 42.0 %shard_map.118 = bf16[12,1280]{1,0:T(8,128)(2,1)S(1)} custom-call(bf16[12,1280]{1,0:T(8,128)(2,1)} %resid_hbm.1, bf16[12,1280]{1,0:T(8,128)(2,1)} %query_hbm.1, bf16[12,512]{1,0:T(8,128)(2,1)} %new_kv_hbm.1, s32[1,48]{1,0:T(1,128)} %bitcast.1, bf16[1280]{0:T(1024)(128)(2,1)} %gain_hbm.1, s32[3]{0:T(128)} %lengths_hbm.1, bf16[3,224,1024]{2,1,0:T(8,128)(2,1)} %keys.1, ...), custom_call_target="tpu_custom_call" | custom-call | tf_op jit(solution)/shard_map/pallas_call | solution.py:799
  42.0 0.6 %copy.14 = bf16[12,1280]{1,0:T(8,128)(2,1)} copy(bf16[12,1280]{1,0:T(8,128)(2,1)S(1)} %shard_map.118) | data formatting | bytes 61440

commit v6 on v5

--- a/solution.py
+++ b/solution.py
@@ -61,7 +61,7 @@
 MESH = pl.DeviceIdType.MESH
 ROWS16 = 16
 HIDDEN_PARTS = 4
-SENDS = 10
+SENDS = 7
 
 
 def up_to(count, multiple):

time: 42.8 us -> 42.6 us (level)
  no operation moved by 1% of the time
where the time goes in v6:
time: 42.6 us; the launch traced here: 42.4 us
  Pallas kernels  41.8 us (98%)
  local copies, waits for them, and re-layouts  0.62 us (1%)
    pallas_call x1, Pallas kernels, fused(): pl.pallas_call(functools.partial(fused_kernel, (S, T, G, R, NH)), out_sha...  41.8 us

profile of v6, /device:TPU:0, one launch (start us, length us, event | category | flops | bytes accessed | tf_op | source)
XLA Modules:
  0.0 42.4 jit_solution(3740920587953094734)
XLA Ops:
  0.0 41.8 %shard_map.118 = bf16[12,1280]{1,0:T(8,128)(2,1)S(1)} custom-call(bf16[12,1280]{1,0:T(8,128)(2,1)} %resid_hbm.1, bf16[12,1280]{1,0:T(8,128)(2,1)} %query_hbm.1, bf16[12,512]{1,0:T(8,128)(2,1)} %new_kv_hbm.1, s32[1,48]{1,0:T(1,128)} %bitcast.1, bf16[1280]{0:T(1024)(128)(2,1)} %gain_hbm.1, s32[3]{0:T(128)} %lengths_hbm.1, bf16[3,224,1024]{2,1,0:T(8,128)(2,1)} %keys.1, ...), custom_call_target="tpu_custom_call" | custom-call | tf_op jit(solution)/shard_map/pallas_call | solution.py:799
  41.8 0.6 %copy.14 = bf16[12,1280]{1,0:T(8,128)(2,1)} copy(bf16[12,1280]{1,0:T(8,128)(2,1)S(1)} %shard_map.118) | data formatting | bytes 61440
